TPU v7x, 32 devices: a whole 2x2x4 slice. The times are simulated.
32 devices in a mesh: wide: 8 (over z, x), narrow: 4 (over y, core).
Axes of the slice: x: 2, y: 2, z: 4, core: 2. Of those that a mesh axis runs over, the one named last changes fastest.
Arguments:
- layer_argument: bfloat16 [20480, 768], P('wide'), may hold values from -6 to 6
- document_extents: int32 [8, 4], P('wide'), may hold values from 1 to 1024, as said below
- distance_bin_lookup: int32 [2047], replicated, may hold values from 0 to 31, as said below
- tile_location: int32 [13], replicated, may hold values from 0 to 15, as said below
- precise_parameter_blocks: float32 [16, 768, 768], P('wide', 'narrow'), may hold values from -0.21875 to 0.21875
- precise_mean_est: float32 [16, 768, 768], P('wide', 'narrow'), may hold values from -2.2888184e-05 to 2.2888184e-05
- precise_variance_est: float32 [16, 768, 768], P('wide', 'narrow'), may hold values from 1.30417e-11 to 5.21668e-11
- rescaling_coefficients: float32 [3, 768], replicated, may hold values from 0.5 to 1.5
- norm_scale_mean_est: float32 [3, 768], replicated, may hold values from -9.1552734e-05 to 9.1552734e-05
- norm_scale_variance_est: float32 [3, 768], replicated, may hold values from 2.086672e-10 to 8.346688e-10
- distance_bias_table: float32 [32, 12], P(None, 'narrow'), may hold values from -6 to 6
- offset_bias_mean_est: float32 [32, 12], P(None, 'narrow'), may hold values from -3.0517578e-05 to 3.0517578e-05
- offset_bias_variance_est: float32 [32, 12], P(None, 'narrow'), may hold values from 1.30417e-11 to 5.21668e-11
- sharpness_exponent: float32 [1], replicated, may hold values from 3 to 3.7
- sharpness_mean_est: float32 [1], replicated, may hold values from -0.03125 to 0.03125
- sharpness_variance_est: float32 [1], replicated, may hold values from 2.5e-05 to 0.0001
Outputs:
- loss: float32 [], replicated
- layer_result: float32 [20480, 768], P('wide')
- input_grad: float32 [20480, 768], P('wide')
- grad_norm: float32 [], replicated
- slot_first: float32 [16, 768, 768], P('wide', 'narrow')
- slot_second: float32 [16, 768, 768], P('wide', 'narrow')
- slot_weight: float32 [16, 768, 768], P('wide', 'narrow')
- gain_first: float32 [3, 768], replicated
- gain_second: float32 [3, 768], replicated
- gain_new: float32 [3, 768], replicated
- bias_first: float32 [32, 12], P(None, 'narrow')
- bias_second: float32 [32, 12], P(None, 'narrow')
- bias_new: float32 [32, 12], P(None, 'narrow')
- sharpness_mean_fresh: float32 [1], replicated
- sharpness_variance_fresh: float32 [1], replicated
- sharpness_exponent_fresh: float32 [1], replicated
Inputs may be any that keep to these rules, and one draw needn't show every extreme that they name: `distance_bin_lookup`: bucket of a relative offset: offsets of size under 32 // 4 have their own buckets, larger ones share buckets that never fall with the offset's size; offsets above zero have 32 // 2 added. Distinct slots; block u belongs to index tile_location[u] // 2 of wide; some index of wide owns 2 blocks. `document_extents`: the lengths of a row add up to 2560.
All inputs are finite; a program needn't handle non-finite values.
Results may differ from a plain program's by a relative error of at most 0.03.
Values may be sent and summed in bfloat16 or wider, within the bound.
No kernel may reach another device: no remote copies, remote signals or barrier semaphores. Data moves between devices by JAX's collectives and lax.ppermute only.
A program may use at most 320 MiB of HBM per device.

v0:
```python
import jax
import jax.numpy as jnp
from jax import lax
from jax.sharding import PartitionSpec as P

D = 768
FF = 3072
BUCKETS = 32
TOK_DEV = 2560
SEQS_DEV = 4
DOCLEN = 1024
QBLOCK = 512
CAP = 2
STEP = 10


norm_eps = 1e-06
clip_limit = 0.01
learn_rate = 0.01
side_rate = 0.5
beta_one = 0.5
beta_two = 0.5
adam_eps = 1e-08
decay_rate = 0.01
score_scale = 0.125
masked_score = -1e30


def times_transposed(left_side, right_side):
    return lax.dot_general(
        left_side, right_side, (((1,), (1,)), ((), ())), preferred_element_type=jnp.float32
    )


def plain_product(left_side, right_side):
    return jnp.dot(left_side, right_side, preferred_element_type=jnp.float32)


def outer_product(left_side, right_side):
    return lax.dot_general(
        left_side, right_side, (((0,), (0,)), ((), ())), preferred_element_type=jnp.float32
    )


def rms_scale(values):
    return lax.rsqrt(jnp.mean(values * values, axis=-1, keepdims=True) + norm_eps)


def norm_backward(values, row_scale, gain_row, grad_out):
    weighted = grad_out * gain_row
    gain_grad = jnp.sum(grad_out * values * row_scale, axis=0)
    inner_mean = jnp.mean(weighted * values, axis=-1, keepdims=True)
    value_grad = row_scale * weighted - values * row_scale * row_scale * row_scale * inner_mean
    return (value_grad, gain_grad)


def toeplitz_rows(extended, row_count, column_count):
    head_count = extended.shape[0]
    full_length = extended.shape[1]
    repeated = jnp.broadcast_to(extended[:, None, :], (head_count, row_count, full_length)).reshape(
        head_count, row_count * full_length
    )
    padded = jnp.pad(repeated, ((0, 0), (0, row_count)))
    shaped = padded.reshape(head_count, row_count, full_length + 1)[:, :, :column_count]
    return shaped[:, ::-1, :]


def diagonal_sums(blocks, row_count, column_count):
    head_count = blocks.shape[0]
    flipped = blocks[:, ::-1, :]
    padded = jnp.pad(flipped, ((0, 0), (0, 0), (0, row_count)))
    flattened = padded.reshape(head_count, row_count * (column_count + row_count))
    flattened = flattened[:, : row_count * (column_count + row_count - 1)]
    skewed = flattened.reshape(head_count, row_count, column_count + row_count - 1)
    return jnp.sum(skewed, axis=1)


def decoupled_decay_step(gradient, first_moment, second_moment, weight, multiplier, step_rate):
    clipped = gradient * multiplier
    first_new = beta_one * first_moment + (1.0 - beta_one) * clipped
    second_new = beta_two * second_moment + (1.0 - beta_two) * clipped * clipped
    first_hat = first_new / (1.0 - beta_one**STEP)
    second_hat = second_new / (1.0 - beta_two**STEP)
    weight_new = weight - step_rate * (
        first_hat / (jnp.sqrt(second_hat) + adam_eps) + decay_rate * weight
    )
    return (first_new, second_new, weight_new)


def on_device(
    layer_argument,
    document_extents,
    distance_bin_lookup,
    tile_location,
    precise_parameter_blocks,
    precise_mean_est,
    precise_variance_est,
    rescaling_coefficients,
    norm_scale_mean_est,
    norm_scale_variance_est,
    distance_bias_table,
    offset_bias_mean_est,
    offset_bias_variance_est,
    sharpness_exponent,
    sharpness_mean_est,
    sharpness_variance_est,
):
    wide_count = lax.axis_size("wide")
    wide_index = lax.axis_index("wide")
    narrow_index = lax.axis_index("narrow")
    unit_rows = precise_parameter_blocks.shape[1]
    heads_here = distance_bias_table.shape[1]
    head_size = unit_rows // heads_here
    ffn_units = FF // D
    window = QBLOCK + 2 * DOCLEN
    block_count = TOK_DEV // QBLOCK
    every_slot = lax.all_gather(
        precise_parameter_blocks.astype(jnp.bfloat16), "wide", axis=0, tiled=True
    ).astype(precise_parameter_blocks.dtype)
    unit_weights = jnp.take(every_slot, tile_location, axis=0)
    weights_low = unit_weights.astype(jnp.bfloat16)
    qkv_weight = weights_low[0:3].reshape(3 * unit_rows, D)
    out_weight = weights_low[3]
    proj_weight = weights_low[4]
    inner_weight = weights_low[5 : 5 + ffn_units].reshape(ffn_units * unit_rows, D)
    outer_weight = weights_low[5 + ffn_units :].reshape(ffn_units * unit_rows, D)
    arguments_list = layer_argument.astype(jnp.float32)
    lengths = document_extents[0]
    seq_ends = jnp.cumsum(lengths)
    positions = jnp.arange(TOK_DEV, dtype=jnp.int32)
    segment_ids = jnp.sum((seq_ends[None, :] <= positions[:, None]).astype(jnp.int32), axis=1)
    segment_padded = jnp.pad(segment_ids, (DOCLEN, DOCLEN), constant_values=-1)
    bucket_onehot = (
        distance_bin_lookup[:, None] == jnp.arange(BUCKETS, dtype=jnp.int32)[None, :]
    ).astype(jnp.float32)
    rel_values = jnp.dot(bucket_onehot, distance_bias_table, precision=lax.Precision.HIGHEST).T
    bias_block = toeplitz_rows(jnp.pad(rel_values, ((0, 0), (QBLOCK, QBLOCK))), QBLOCK, window)
    scale_one = rms_scale(arguments_list)
    normed_one = (arguments_list * scale_one * rescaling_coefficients[0]).astype(jnp.bfloat16)
    projections = times_transposed(normed_one, qkv_weight).astype(jnp.bfloat16)
    query_rows = projections[:, :unit_rows]
    key_padded = jnp.pad(projections[:, unit_rows : 2 * unit_rows], ((DOCLEN, DOCLEN), (0, 0)))
    value_padded = jnp.pad(projections[:, 2 * unit_rows :], ((DOCLEN, DOCLEN), (0, 0)))

    def block_scores(block_start):
        query_block = lax.dynamic_slice_in_dim(query_rows, block_start, QBLOCK, 0).reshape(
            QBLOCK, heads_here, head_size
        )
        key_block = lax.dynamic_slice_in_dim(key_padded, block_start, window, 0).reshape(
            window, heads_here, head_size
        )
        value_block = lax.dynamic_slice_in_dim(value_padded, block_start, window, 0).reshape(
            window, heads_here, head_size
        )
        scores = (
            jnp.einsum("qhd,khd->hqk", query_block, key_block, preferred_element_type=jnp.float32)
            * score_scale
            + bias_block
        )
        query_segments = lax.dynamic_slice_in_dim(segment_ids, block_start, QBLOCK, 0)
        key_segments = lax.dynamic_slice_in_dim(segment_padded, block_start, window, 0)
        allowed = query_segments[:, None] == key_segments[None, :]
        scores = jnp.where(allowed[None, :, :], scores, masked_score)
        return (scores, query_block, key_block, value_block)

    def forward_block(state_in, block_index):
        block_start = block_index * QBLOCK
        scores, query_block, key_block, value_block = block_scores(block_start)
        row_top = jnp.max(scores, axis=-1, keepdims=True)
        weights = jnp.exp(scores - row_top)
        row_total = jnp.sum(weights, axis=-1, keepdims=True)
        probabilities = (weights / row_total).astype(jnp.bfloat16)
        context_block = jnp.einsum(
            "hqk,khd->qhd", probabilities, value_block, preferred_element_type=jnp.float32
        )
        return (state_in, (context_block.reshape(QBLOCK, unit_rows), row_top + jnp.log(row_total)))

    state_out, (context_blocks, log_blocks) = lax.scan(
        forward_block, jnp.zeros((), jnp.float32), jnp.arange(block_count, dtype=jnp.int32)
    )
    context = context_blocks.reshape(TOK_DEV, unit_rows).astype(jnp.bfloat16)
    attn_total = lax.psum(plain_product(context, out_weight), "narrow")
    residual_mid = arguments_list + attn_total
    scale_two = rms_scale(residual_mid)
    normed_two = (residual_mid * scale_two * rescaling_coefficients[1]).astype(jnp.bfloat16)
    gate_pre = times_transposed(normed_two, inner_weight)
    hidden_act, gelu_back = jax.vjp(jax.nn.gelu, gate_pre)
    hidden_low = hidden_act.astype(jnp.bfloat16)
    ffn_total = lax.psum(plain_product(hidden_low, outer_weight), "narrow")
    layer_result = residual_mid + ffn_total
    scale_three = rms_scale(layer_result)
    final_rows = layer_result * scale_three * rescaling_coefficients[2]
    member = (segment_ids[None, :] == jnp.arange(SEQS_DEV, dtype=jnp.int32)[:, None]).astype(
        jnp.float32
    )
    length_values = lengths.astype(jnp.float32)[:, None]
    pooled = jnp.dot(member, final_rows, precision=lax.Precision.HIGHEST) / length_values
    pooled_low = pooled.astype(jnp.bfloat16)
    proj_part = times_transposed(pooled_low, proj_weight).astype(jnp.bfloat16)
    projected = lax.all_gather(proj_part, "narrow", axis=1, tiled=True).astype(jnp.float32)
    inverse = lax.rsqrt(jnp.sum(projected * projected, axis=1, keepdims=True) + norm_eps)
    embed_low = (projected * inverse).astype(jnp.bfloat16)
    every_low = lax.all_gather(embed_low, "wide", axis=0, tiled=True)
    gathered_embeddings = every_low.astype(jnp.float32)
    embed_own = embed_low.astype(jnp.float32)
    sharpness_factor = jnp.exp(sharpness_exponent[0])
    angular_agreement = times_transposed(embed_low, every_low)
    sharpened_agreement = sharpness_factor * angular_agreement
    global_rows = wide_index * SEQS_DEV + jnp.arange(SEQS_DEV, dtype=jnp.int32)
    columns = jnp.arange(gathered_embeddings.shape[0], dtype=jnp.int32)
    sharpened_agreement = jnp.where(
        columns[None, :] == global_rows[:, None], masked_score, sharpened_agreement
    )
    row_top = jnp.max(sharpened_agreement, axis=1, keepdims=True)
    log_total = row_top + jnp.log(
        jnp.sum(jnp.exp(sharpened_agreement - row_top), axis=1, keepdims=True)
    )
    partner = jnp.bitwise_xor(global_rows, 1)
    positive_mask = (columns[None, :] == partner[:, None]).astype(jnp.float32)
    positive = jnp.sum(
        positive_mask * jnp.where(positive_mask > 0.0, sharpened_agreement, 0.0), axis=1
    )
    total_seqs = gathered_embeddings.shape[0]
    penalty_piece = jnp.sum(log_total[:, 0] - positive) / total_seqs
    softmax_rows = jnp.exp(sharpened_agreement - log_total)
    raw_score_slope = (softmax_rows - positive_mask) / total_seqs
    sharpness_derivative = sharpness_factor * jnp.sum(raw_score_slope * angular_agreement)
    horizontal_penalty_slope = sharpness_factor * jnp.dot(
        raw_score_slope, gathered_embeddings, precision=lax.Precision.HIGHEST
    )
    vertical_penalty_piece = sharpness_factor * lax.dot_general(
        raw_score_slope, embed_own, (((0,), (0,)), ((), ())), precision=lax.Precision.HIGHEST
    )
    embed_grad = horizontal_penalty_slope + lax.psum_scatter(
        vertical_penalty_piece, "wide", scatter_dimension=0, tiled=True
    )
    along = jnp.sum(projected * embed_grad, axis=1, keepdims=True)
    proj_grad = inverse * embed_grad - projected * inverse * inverse * inverse * along
    proj_grad_low = lax.dynamic_slice_in_dim(
        proj_grad, narrow_index * unit_rows, unit_rows, 1
    ).astype(jnp.bfloat16)
    proj_weight_grad = outer_product(proj_grad_low, pooled_low)
    pooled_grad = lax.psum(plain_product(proj_grad_low, proj_weight), "narrow")
    final_grad = lax.dot_general(
        member,
        pooled_grad / length_values,
        (((0,), (0,)), ((), ())),
        precision=lax.Precision.HIGHEST,
    )
    encoded_grad, final_gain_grad = norm_backward(
        layer_result, scale_three, rescaling_coefficients[2], final_grad
    )
    ffn_grad_low = encoded_grad.astype(jnp.bfloat16)
    hidden_grad = times_transposed(ffn_grad_low, outer_weight)
    outer_grad = outer_product(hidden_low, ffn_grad_low)
    (pre_grad,) = gelu_back(hidden_grad)
    pre_low = pre_grad.astype(jnp.bfloat16)
    inner_grad = outer_product(pre_low, normed_two)
    normed_two_grad = lax.psum(plain_product(pre_low, inner_weight), "narrow")
    mid_norm_grad, ffn_gain_grad = norm_backward(
        residual_mid, scale_two, rescaling_coefficients[1], normed_two_grad
    )
    mid_grad = encoded_grad + mid_norm_grad
    attn_grad_low = mid_grad.astype(jnp.bfloat16)
    context_grad = times_transposed(attn_grad_low, out_weight).astype(jnp.bfloat16)
    out_grad = outer_product(context, attn_grad_low)

    def backward_block(state_in, block_index):
        key_acc, value_acc, score_acc = state_in
        block_start = block_index * QBLOCK
        scores, query_block, key_block, value_block = block_scores(block_start)
        probabilities = jnp.exp(scores - log_blocks[block_index])
        context_block = lax.dynamic_slice_in_dim(context_grad, block_start, QBLOCK, 0).reshape(
            QBLOCK, heads_here, head_size
        )
        prob_grad = jnp.einsum(
            "qhd,khd->hqk", context_block, value_block, preferred_element_type=jnp.float32
        )
        row_delta = jnp.sum(probabilities * prob_grad, axis=-1, keepdims=True)
        score_grad = (probabilities * (prob_grad - row_delta)).astype(jnp.bfloat16)
        value_part = jnp.einsum(
            "hqk,qhd->khd",
            probabilities.astype(jnp.bfloat16),
            context_block,
            preferred_element_type=jnp.float32,
        )
        query_part = (
            jnp.einsum("hqk,khd->qhd", score_grad, key_block, preferred_element_type=jnp.float32)
            * score_scale
        )
        key_part = (
            jnp.einsum("hqk,qhd->khd", score_grad, query_block, preferred_element_type=jnp.float32)
            * score_scale
        )
        key_old = lax.dynamic_slice_in_dim(key_acc, block_start, window, 0)
        key_acc = lax.dynamic_update_slice_in_dim(
            key_acc, key_old + key_part.reshape(window, unit_rows), block_start, 0
        )
        value_old = lax.dynamic_slice_in_dim(value_acc, block_start, window, 0)
        value_acc = lax.dynamic_update_slice_in_dim(
            value_acc, value_old + value_part.reshape(window, unit_rows), block_start, 0
        )
        score_acc = score_acc + score_grad.astype(jnp.float32)
        return ((key_acc, value_acc, score_acc), query_part.reshape(QBLOCK, unit_rows))

    empty_rows = jnp.zeros((TOK_DEV + 2 * DOCLEN, unit_rows), jnp.float32)
    empty_scores = jnp.zeros((heads_here, QBLOCK, window), jnp.float32)
    (key_acc, value_acc, score_acc), query_blocks = lax.scan(
        backward_block,
        (empty_rows, empty_rows, empty_scores),
        jnp.arange(block_count, dtype=jnp.int32),
    )
    qkv_low = jnp.concatenate(
        [
            query_blocks.reshape(TOK_DEV, unit_rows),
            key_acc[DOCLEN : DOCLEN + TOK_DEV],
            value_acc[DOCLEN : DOCLEN + TOK_DEV],
        ],
        axis=1,
    ).astype(jnp.bfloat16)
    diagonals = diagonal_sums(score_acc, QBLOCK, window)
    rel_grad = diagonals[:, QBLOCK : QBLOCK + 2 * DOCLEN - 1]
    offset_bias_slope = lax.dot_general(
        bucket_onehot, rel_grad, (((0,), (1,)), ((), ())), precision=lax.Precision.HIGHEST
    )
    qkv_weight_grad = outer_product(qkv_low, normed_one)
    normed_one_grad = lax.psum(plain_product(qkv_low, qkv_weight), "narrow")
    input_norm_grad, attn_gain_grad = norm_backward(
        arguments_list, scale_one, rescaling_coefficients[0], normed_one_grad
    )
    input_grad = mid_grad + input_norm_grad
    unit_grads = jnp.concatenate(
        [
            qkv_weight_grad.reshape(3, unit_rows, D),
            out_grad[None],
            proj_weight_grad[None],
            inner_grad.reshape(ffn_units, unit_rows, D),
            outer_grad.reshape(ffn_units, unit_rows, D),
        ],
        axis=0,
    )
    norm_scale_slopes = jnp.stack([attn_gain_grad, ffn_gain_grad, final_gain_grad])
    gain_total, bias_total, sharpness_slope_overall, loss_total = lax.psum(
        (
            norm_scale_slopes,
            offset_bias_slope,
            sharpness_derivative.reshape(1),
            penalty_piece.reshape(1),
        ),
        "wide",
    )
    placed = (
        jnp.zeros((wide_count * CAP,) + precise_parameter_blocks.shape[1:], jnp.float32)
        .at[tile_location]
        .set(unit_grads)
    )
    slot_grads = lax.psum_scatter(placed, "wide", scatter_dimension=0, tiled=True)
    first_wide = (wide_index == 0).astype(jnp.float32)
    first_both = first_wide * (narrow_index == 0).astype(jnp.float32)
    local_squares = (
        jnp.sum(slot_grads * slot_grads)
        + first_wide * jnp.sum(bias_total * bias_total)
        + first_both
        * (
            jnp.sum(gain_total * gain_total)
            + jnp.sum(sharpness_slope_overall * sharpness_slope_overall)
        )
    )
    grad_norm = jnp.sqrt(lax.psum(local_squares, ("wide", "narrow")))
    multiplier = jnp.minimum(1.0, clip_limit / grad_norm)
    slot_first, slot_second, slot_weight = decoupled_decay_step(
        slot_grads,
        precise_mean_est,
        precise_variance_est,
        precise_parameter_blocks,
        multiplier,
        learn_rate,
    )
    gain_first, gain_second, gain_new = decoupled_decay_step(
        gain_total,
        norm_scale_mean_est,
        norm_scale_variance_est,
        rescaling_coefficients,
        multiplier,
        side_rate,
    )
    bias_first, bias_second, bias_new = decoupled_decay_step(
        bias_total,
        offset_bias_mean_est,
        offset_bias_variance_est,
        distance_bias_table,
        multiplier,
        side_rate,
    )
    sharpness_mean_fresh, sharpness_variance_fresh, sharpness_exponent_fresh = decoupled_decay_step(
        sharpness_slope_overall,
        sharpness_mean_est,
        sharpness_variance_est,
        sharpness_exponent,
        multiplier,
        learn_rate,
    )
    return (
        loss_total[0],
        layer_result,
        input_grad,
        grad_norm,
        slot_first,
        slot_second,
        slot_weight,
        gain_first,
        gain_second,
        gain_new,
        bias_first,
        bias_second,
        bias_new,
        sharpness_mean_fresh,
        sharpness_variance_fresh,
        sharpness_exponent_fresh,
    )


def solution(mesh):
    placed = (
        P("wide", None),
        P("wide", None),
        P(),
        P(),
        P("wide", "narrow", None),
        P("wide", "narrow", None),
        P("wide", "narrow", None),
        P(),
        P(),
        P(),
        P(None, "narrow"),
        P(None, "narrow"),
        P(None, "narrow"),
        P(),
        P(),
        P(),
    )
    return jax.shard_map(
        on_device,
        mesh=mesh,
        in_specs=placed,
        out_specs=(
            P(),
            P("wide", None),
            P("wide", None),
            P(),
            P("wide", "narrow", None),
            P("wide", "narrow", None),
            P("wide", "narrow", None),
            P(),
            P(),
            P(),
            P(None, "narrow"),
            P(None, "narrow"),
            P(None, "narrow"),
            P(),
            P(),
            P(),
        ),
        check_vma=False,
    )
```

profile of v0, /device:TPU:0, one launch (start us, length us, event | category | flops | bytes accessed | tf_op | source)
XLA Modules:
  0.0 2503.8 jit_solution(11565600787225560666)
XLA Ops:
  11.7 8.8 broadcast_in_dim.107
  20.5 26.6 %reshape.334 = f32[4717056]{0:T(1024)} reshape(f32[3,512,3071]{2,1,0:T(8,128)} %broadcast_in_dim.107) | data formatting | bytes 37736448
  47.2 371.4 %while.33 = (u32[]{:T(128)}, f32[4717056]{0:T(1024)}, f32[1,3,1572352]{2,1,0:T(4,128)}, u32[]{}, u32[]{}, /*index=5*/u32[]{}, u32[]{}, u32[]{}) while((u32[]{:T(128)}, f32[4717056]{0:T(1024)}, f32[1,3,1572352]{2,1,0:T(4,128)}, u32[]{}, u32[]{}, /*index=5*/u32[]{}, u32[]{}, u32[]{}) %tuple.95), condition=%wide.cond, body=%wide.body.sunk | while | flops 9 | bytes 37736624
  58.3 113.1 %dynamic-update-slice.14 = f32[1,3,1572352]{2,1,0:T(4,128)} dynamic-update-slice(f32[1,3,1572352]{2,1,0:T(4,128)} %get-tuple-element.529, f32[1,1,1572352]{2,1,0:T(1,128)} %reshape.339, u32[]{:T(128)S(6)} %multiply.66, u32[]{:T(128)S(6)} %multiply.68, u32[]{} %constant.318..sunk) | dynamic-update-slice | bytes 12578820
  181.9 113.0 %dynamic-update-slice.14 = f32[1,3,1572352]{2,1,0:T(4,128)} dynamic-update-slice(f32[1,3,1572352]{2,1,0:T(4,128)} %get-tuple-element.529, f32[1,1,1572352]{2,1,0:T(1,128)} %reshape.339, u32[]{:T(128)S(6)} %multiply.66, u32[]{:T(128)S(6)} %multiply.68, u32[]{} %constant.318..sunk) | dynamic-update-slice | bytes 12578820
  305.6 113.0 %dynamic-update-slice.14 = f32[1,3,1572352]{2,1,0:T(4,128)} dynamic-update-slice(f32[1,3,1572352]{2,1,0:T(4,128)} %get-tuple-element.529, f32[1,1,1572352]{2,1,0:T(1,128)} %reshape.339, u32[]{:T(128)S(6)} %multiply.66, u32[]{:T(128)S(6)} %multiply.68, u32[]{} %constant.318..sunk) | dynamic-update-slice | bytes 12578820
  418.6 13.2 pad.27
  431.8 13.4 copy.54
  445.2 12.3 slice.75
  457.6 120.0 %rev.6 = f32[3,512,2560]{2,1,0:T(8,128)} reverse(f32[3,512,2560]{2,1,0:T(8,128)} %slice.75), dimensions={1} | reverse | bytes 31457280 | tf_op jit(solution)/shard_map/rev | solution.py:65
  595.1 150.2 %while.31 = (s32[]{:T(128)}, bf16[5,512,192]{1,2,0:T(8,128)(2,1)}, f32[5,3,512,1]{2,1,3,0:T(4,128)S(1)}, s32[5]{0:T(128)S(1)}, bf16[4608,192]{0,1:T(8,128)(2,1)}...) while((s32[]{:T(128)}, bf16[5,512,192]{1,2,0:T(8,128)(2,1)}, ...), condition=%wide.region_6.7_spmd, body=%wide.region_3.6_spmd.sunk | while | flops 1043331584 | bytes 72706800 | solution.py:178
  599.1 10.9 fusion.145
  610.1 7.7 fusion.146
  629.1 10.9 fusion.145
  640.0 7.7 fusion.146
  659.0 10.9 fusion.145
  670.0 7.7 fusion.146
  689.0 10.9 fusion.145
  700.0 7.7 fusion.146
  719.0 10.9 fusion.145
  729.9 7.7 fusion.146
  756.1 146.0 %all-reduce.14.cloned.1.call-done = f32[2560,768]{1,0:T(8,128)} async-done(((f32[2560,768]{1,0:T(8,128)}), f32[2560,768]{1,0:T(8,128)}) %all-reduce.14.cloned.1.call-update) | async-done | bytes 7864336 | tf_op jit(solution)/shard_map/psum | solution.py:182
  921.9 144.8 %all-reduce.16.cloned.1.call-done = f32[2560,768]{1,0:T(8,128)} async-done(((f32[2560,768]{1,0:T(8,128)}), f32[2560,768]{1,0:T(8,128)}) %all-reduce.16.cloned.1.call-update) | async-done | bytes 7864336 | tf_op jit(solution)/shard_map/psum | solution.py:189
  1086.2 30.7 %all-gather.1 = bf16[8,4,768]{2,1,0:T(4,128)(2,1)S(1)} all-gather(bf16[1,4,768]{2,1,0:T(4,128)(2,1)S(1)} %get-tuple-element.291), channel_id=1, replica_groups=mesh['wide'=8,'narrow'=4] {'wide'}, dimensions={0}, use_global_device_ids=true | all-gather | bytes 55296 | tf_op jit(solution)/shard_map/all_gather | solution.py:203
  1119.7 68.4 %all-reduce.22.cloned.1.call-done = f32[32,768]{1,0:T(8,128)} async-done(((f32[32,768]{1,0:T(8,128)}), f32[32,768]{1,0:T(8,128)}) %all-reduce.22.cloned.1.call-update) | async-done | bytes 98320
  1190.3 10.5 psum.73
  1200.9 8.0 multiply_reduce_fusion.1
  1213.6 7.5 fusion.17
  1233.1 10.1 fusion.84
  1243.1 129.9 %all-reduce.18.cloned.1.call-done = f32[2560,768]{1,0:T(8,128)} async-done(((f32[2560,768]{1,0:T(8,128)}), f32[2560,768]{1,0:T(8,128)}) %all-reduce.18.cloned.1.call-update) | async-done | bytes 7864336 | tf_op jit(solution)/shard_map/psum | solution.py:259
  1373.1 7.4 multiply_reduce_fusion.2
  1396.7 359.0 %while.32 = (s32[]{:T(128)}, f32[4608,192]{0,1:T(8,128)}, f32[4608,192]{0,1:T(8,128)}, f32[3,512,2560]{2,1,0:T(8,128)}, bf16[5,512,192]{1,2,0:T(8,128)(2,1)}, /*...) while((s32[]{:T(128)}, f32[4608,192]{0,1:T(8,128)}, ...), condition=%wide.region_25.26_spmd.clone, body=%wide.region_23.25_spmd.clone.sunk | while | flops 2570680832 | bytes 270470144 | solution.py:308
  1400.4 7.7 fusion.158
  1412.0 17.1 multiply_reduce_fusion.12
  1429.1 20.6 select_add_fusion.2
  1468.2 7.7 fusion.158
  1479.9 17.1 multiply_reduce_fusion.12
  1497.0 25.4 %select_add_fusion.2 = (f32[3,512,2560]{2,1,0:T(8,128)}, bf16[3,512,2560]{2,1,0:T(8,128)(2,1)}) fusion(f32[3,512,2560]{2,1,0:T(8,128)} %get-tuple-element.611, pred[]{:T(512)S(6)} %compare.13, f32[3,512,2560]{2,1,0:T(8,128)} %get-tuple-element.507, f32[3,512,2560]{2,1,0:T(8,128)} %fusion.158, f32[3,512]{1,0:T(4,128)S(1)} %get-tuple-element.508), kind=kLoop, calls=%fused_computation.13.clone.1 | loop fusion | flops 23592960 | bytes 70785024 | tf_op jit(solution)/shard_map/while/body/eval_jaxpr/add | solution.py:303
  1541.0 7.7 fusion.158
  1552.6 17.1 multiply_reduce_fusion.12
  1569.8 25.4 %select_add_fusion.2 = (f32[3,512,2560]{2,1,0:T(8,128)}, bf16[3,512,2560]{2,1,0:T(8,128)(2,1)}) fusion(f32[3,512,2560]{2,1,0:T(8,128)} %get-tuple-element.611, pred[]{:T(512)S(6)} %compare.13, f32[3,512,2560]{2,1,0:T(8,128)} %get-tuple-element.507, f32[3,512,2560]{2,1,0:T(8,128)} %fusion.158, f32[3,512]{1,0:T(4,128)S(1)} %get-tuple-element.508), kind=kLoop, calls=%fused_computation.13.clone.1 | loop fusion | flops 23592960 | bytes 70785024 | tf_op jit(solution)/shard_map/while/body/eval_jaxpr/add | solution.py:303
  1613.7 7.7 fusion.158
  1625.4 17.1 multiply_reduce_fusion.12
  1642.5 25.4 %select_add_fusion.2 = (f32[3,512,2560]{2,1,0:T(8,128)}, bf16[3,512,2560]{2,1,0:T(8,128)(2,1)}) fusion(f32[3,512,2560]{2,1,0:T(8,128)} %get-tuple-element.611, pred[]{:T(512)S(6)} %compare.13, f32[3,512,2560]{2,1,0:T(8,128)} %get-tuple-element.507, f32[3,512,2560]{2,1,0:T(8,128)} %fusion.158, f32[3,512]{1,0:T(4,128)S(1)} %get-tuple-element.508), kind=kLoop, calls=%fused_computation.13.clone.1 | loop fusion | flops 23592960 | bytes 70785024 | tf_op jit(solution)/shard_map/while/body/eval_jaxpr/add | solution.py:303
  1686.5 7.7 fusion.158
  1698.1 17.1 multiply_reduce_fusion.12
  1715.2 25.4 %select_add_fusion.2 = (f32[3,512,2560]{2,1,0:T(8,128)}, bf16[3,512,2560]{2,1,0:T(8,128)(2,1)}) fusion(f32[3,512,2560]{2,1,0:T(8,128)} %get-tuple-element.611, pred[]{:T(512)S(6)} %compare.13, f32[3,512,2560]{2,1,0:T(8,128)} %get-tuple-element.507, f32[3,512,2560]{2,1,0:T(8,128)} %fusion.158, f32[3,512]{1,0:T(4,128)S(1)} %get-tuple-element.508), kind=kLoop, calls=%fused_computation.13.clone.1 | loop fusion | flops 23592960 | bytes 70785024 | tf_op jit(solution)/shard_map/while/body/eval_jaxpr/add | solution.py:303
  1768.5 8.5 fusion.30
  1777.0 120.2 %rev.7 = f32[3,512,2560]{2,1,0:T(8,128)} reverse(f32[3,512,2560]{2,1,0:T(8,128)} %get-tuple-element.149), dimensions={1} | reverse | bytes 31457280 | tf_op jit(solution)/shard_map/rev | solution.py:70
  1904.1 37.4 %copy.52 = f32[1,3,512,3072]{3,1,2,0:T(4,128)} copy(f32[1,3,512,3072]{3,2,1,0:T(8,128)S(1)} %pad_bitcast_fusion) | data formatting | bytes 37748736
  1957.7 15.2 scatter_fusion
  1973.0 21.7 slice_bitcast_fusion.6
  1994.7 354.8 %while.34 = (u32[]{:T(128)}, f32[1,3,1572352]{2,1,0:T(4,128)}, f32[4717056]{0:T(1024)}, u32[]{}, f32[]{:T(128)}, /*index=5*/u32[]{}, u32[]{}, u32[]{}) while((u32[]{:T(128)}, f32[1,3,1572352]{2,1,0:T(4,128)}, f32[4717056]{0:T(1024)}, u32[]{}, f32[]{:T(128)}, /*index=5*/u32[]{}, u32[]{}, u32[]{}) %tuple.104), condition=%wide.cond.1, body=%wide.body.1.sunk | while | flops 9 | bytes 25157824
  1995.4 63.6 %dynamic-slice_reduce_fusion.2 = f32[1572352]{0:T(1024)} fusion(f32[]{:T(128)} %broadcast.304, f32[1,3,1572352]{2,1,0:T(4,128)} %get-tuple-element.665, u32[]{:T(128)S(6)} %multiply.70, u32[]{:T(128)S(6)} %multiply.71), kind=kLoop, calls=%fused_computation.188.clone.1 | loop fusion | bytes 12578828
  2059.0 54.3 %dynamic-update-slice.15 = f32[4717056]{0:T(1024)} dynamic-update-slice(f32[4717056]{0:T(1024)} %get-tuple-element.658, f32[1572352]{0:T(1024)} %dynamic-slice_reduce_fusion.2, u32[]{:T(128)S(6)} %add.391) | dynamic-update-slice | bytes 12578820
  2113.8 63.6 %dynamic-slice_reduce_fusion.2 = f32[1572352]{0:T(1024)} fusion(f32[]{:T(128)} %broadcast.304, f32[1,3,1572352]{2,1,0:T(4,128)} %get-tuple-element.665, u32[]{:T(128)S(6)} %multiply.70, u32[]{:T(128)S(6)} %multiply.71), kind=kLoop, calls=%fused_computation.188.clone.1 | loop fusion | bytes 12578828
  2177.4 54.2 %dynamic-update-slice.15 = f32[4717056]{0:T(1024)} dynamic-update-slice(f32[4717056]{0:T(1024)} %get-tuple-element.658, f32[1572352]{0:T(1024)} %dynamic-slice_reduce_fusion.2, u32[]{:T(128)S(6)} %add.391) | dynamic-update-slice | bytes 12578820
  2232.2 63.6 %dynamic-slice_reduce_fusion.2 = f32[1572352]{0:T(1024)} fusion(f32[]{:T(128)} %broadcast.304, f32[1,3,1572352]{2,1,0:T(4,128)} %get-tuple-element.665, u32[]{:T(128)S(6)} %multiply.70, u32[]{:T(128)S(6)} %multiply.71), kind=kLoop, calls=%fused_computation.188.clone.1 | loop fusion | bytes 12578828
  2295.8 53.8 %dynamic-update-slice.15 = f32[4717056]{0:T(1024)} dynamic-update-slice(f32[4717056]{0:T(1024)} %get-tuple-element.658, f32[1572352]{0:T(1024)} %dynamic-slice_reduce_fusion.2, u32[]{:T(128)S(6)} %add.391) | dynamic-update-slice | bytes 12578820
  2349.5 26.9 %reshape.298 = f32[3,512,3071]{2,1,0:T(8,128)} reshape(f32[4717056]{0:T(1024)} %get-tuple-element.204) | data formatting | bytes 37736448 | tf_op jit(solution)/shard_map/reshape | solution.py:74
  2376.4 7.4 reduce_sum.217
  2390.5 38.2 %all-reduce.7 = (f32[]{:T(128)}, f32[32,3]{0,1:T(4,128)S(1)}, f32[3,768]{1,0:T(4,128)S(1)}, f32[1]{0:T(128)}) all-reduce(f32[]{:T(128)S(6)} %div.93, f32[32,3]{0,1:T(4,128)S(1)} %fusion.56, f32[3,768]{1,0:T(4,128)S(1)} %pad_maximum_fusion.3, f32[1]{0:T(128)} %bitcast.28), channel_id=1, replica_groups=mesh['wide'=8,'narrow'=4] {'wide'}, use_global_device_ids=true, to_apply=%region_16.17 | all-reduce | flops 2402 | bytes 19216 | tf_op jit(solution)/shard_map/psum | solution.py:343
  2436.0 11.3 fusion.10
  2447.3 36.8 %psum.79 = f32[]{:T(128)} all-reduce(f32[]{:T(128)S(6)} %add.266), channel_id=1, replica_groups=mesh['wide'=8,'narrow'=4] {'wide','narrow'}, use_global_device_ids=true, to_apply=%region_41.42 | all-reduce | flops 1 | bytes 8 | tf_op jit(solution)/shard_map/psum | solution.py:369
  (417 shorter events, 344.6 us)
Async XLA Ops:
  7.2 574.2 %all-gather.4.cloned.1.call-start = ((), (), s32[]{:S(2)}) async-start(), calls=%async_computation.1 | async-start | bytes 5308416 | tf_op jit(solution)/shard_map/all_gather | solution.py:117
  9.4 892.7 %all-reduce.14.cloned.1.call-start = ((), (), s32[]{:S(2)}) async-start(), calls=%async_computation.2 | async-start | bytes 15728640 | tf_op jit(solution)/shard_map/psum | solution.py:182
  457.6 120.2 %copy-start.44 = (s32[13]{0:T(128)S(1)}, s32[13]{0:T(128)}, u32[]{:S(2)}) copy-start(s32[13]{0:T(128)} %param.23) | copy-start | bytes 160
  457.6 120.2 %copy-start.33 = (f32[3,768]{1,0:T(4,128)S(1)}, f32[3,768]{1,0:T(4,128)}, u32[]{:S(2)}) copy-start(f32[3,768]{1,0:T(4,128)} %param.27) | copy-start | bytes 27652
  578.4 11.4 copy-start.34
  581.4 8.4 copy-start.26
  746.3 7.7 copy-start.3
  754.0 312.6 %all-reduce.16.cloned.1.call-start = ((), (), s32[]{:S(2)}) async-start(), calls=%async_computation.3 | async-start | bytes 15728640 | tf_op jit(solution)/shard_map/psum | solution.py:189
  756.0 151.5 %copy-start.18 = (bf16[4,192,768]{2,1,0:T(8,128)(2,1)}, bf16[4,192,768]{2,1,0:T(8,128)(2,1)S(1)}, u32[]{:S(2)}) copy-start(bf16[4,192,768]{2,1,0:T(8,128)(2,1)S(1)} %get-tuple-element.305) | copy-start | bytes 3538948
  756.0 155.0 %copy-start.20 = (bf16[4,192,768]{2,1,0:T(8,128)(2,1)}, bf16[4,192,768]{2,1,0:T(8,128)(2,1)S(1)}, u32[]{:S(2)}) copy-start(bf16[4,192,768]{2,1,0:T(8,128)(2,1)S(1)} %get-tuple-element.306) | copy-start | bytes 3538948
  756.0 151.5 %copy-start.29 = (f32[768]{0:T(1024)S(1)}, f32[768]{0:T(1024)}, u32[]{:S(2)}) copy-start(f32[768]{0:T(1024)} %get-tuple-element.212) | copy-start | bytes 9220
  921.1 267.0 %all-reduce.22.cloned.1.call-start = ((), (), s32[]{:S(2)}) async-start(), calls=%async_computation.7 | async-start | bytes 196608
  921.9 154.4 %copy-start.28 = (f32[768]{0:T(1024)S(1)}, f32[768]{0:T(1024)}, u32[]{:S(2)}) copy-start(f32[768]{0:T(1024)} %get-tuple-element.211) | copy-start | bytes 9220
  1073.1 45.4 %copy-start.46 = (u32[32]{0:T(128)S(1)}, u32[32]{0:T(128)}, u32[]{:S(2)}) copy-start(u32[32]{0:T(128)} %constant.189) | copy-start | bytes 388
  1118.4 254.7 %all-reduce.18.cloned.1.call-start = ((), (), s32[]{:S(2)}) async-start(), calls=%async_computation.4 | async-start | bytes 15728640 | tf_op jit(solution)/shard_map/psum | solution.py:259
  1189.2 19.7 copy-start.36
  1200.9 12.6 slice-start.8
  1213.6 7.5 copy-start.8
  1213.6 9.5 copy-start.19
  1228.5 1155.9 %all-reduce.20.cloned.1.call-start = ((), (), s32[]{:S(2)}) async-start(), calls=%async_computation.5 | async-start | bytes 15728640 | tf_op jit(solution)/shard_map/psum | solution.py:327
  1373.1 7.8 copy-start.7
  1400.4 8.7 copy-start.4
  1429.1 26.3 %slice-start = ((s8[15728640]{0:T(1024)(128)(4,1)}), s8[4194304]{0:T(1024)(128)(4,1)S(1)}, s32[]{:S(2)}) async-start(s8[15728640]{0:T(1024)(128)(4,1)} %bitcast.168), calls=%async_computation.8 | async-start | bytes 8388608 | tf_op jit(solution)/shard_map/while
  1429.1 26.3 %slice-start.1 = ((s8[15728640]{0:T(1024)(128)(4,1)}), s8[4194304]{0:T(1024)(128)(4,1)S(1)}, s32[]{:S(2)}) async-start(s8[15728640]{0:T(1024)(128)(4,1)} %bitcast.168), calls=%async_computation.9 | async-start | bytes 8388608 | tf_op jit(solution)/shard_map/while
  1429.1 26.4 %slice-start.2 = ((s8[15728640]{0:T(1024)(128)(4,1)}), s8[4194304]{0:T(1024)(128)(4,1)S(1)}, s32[]{:S(2)}) async-start(s8[15728640]{0:T(1024)(128)(4,1)} %bitcast.168), calls=%async_computation.10 | async-start | bytes 8388608 | tf_op jit(solution)/shard_map/while
  1429.1 26.3 %slice-start.3 = ((s8[15728640]{0:T(1024)(128)(4,1)}), s8[3145728]{0:T(1024)(128)(4,1)S(1)}, s32[]{:S(2)}) async-start(s8[15728640]{0:T(1024)(128)(4,1)} %bitcast.168), calls=%async_computation.11 | async-start | bytes 6291456 | tf_op jit(solution)/shard_map/while
  1449.8 11.8 slice-start.4
  1468.2 8.7 copy-start.4
  1497.0 31.2 %slice-start = ((s8[15728640]{0:T(1024)(128)(4,1)}), s8[4194304]{0:T(1024)(128)(4,1)S(1)}, s32[]{:S(2)}) async-start(s8[15728640]{0:T(1024)(128)(4,1)} %bitcast.168), calls=%async_computation.8 | async-start | bytes 8388608 | tf_op jit(solution)/shard_map/while
  1497.0 31.2 %slice-start.1 = ((s8[15728640]{0:T(1024)(128)(4,1)}), s8[4194304]{0:T(1024)(128)(4,1)S(1)}, s32[]{:S(2)}) async-start(s8[15728640]{0:T(1024)(128)(4,1)} %bitcast.168), calls=%async_computation.9 | async-start | bytes 8388608 | tf_op jit(solution)/shard_map/while
  1497.0 31.2 %slice-start.2 = ((s8[15728640]{0:T(1024)(128)(4,1)}), s8[4194304]{0:T(1024)(128)(4,1)S(1)}, s32[]{:S(2)}) async-start(s8[15728640]{0:T(1024)(128)(4,1)} %bitcast.168), calls=%async_computation.10 | async-start | bytes 8388608 | tf_op jit(solution)/shard_map/while
  1497.0 31.2 %slice-start.3 = ((s8[15728640]{0:T(1024)(128)(4,1)}), s8[3145728]{0:T(1024)(128)(4,1)S(1)}, s32[]{:S(2)}) async-start(s8[15728640]{0:T(1024)(128)(4,1)} %bitcast.168), calls=%async_computation.11 | async-start | bytes 6291456 | tf_op jit(solution)/shard_map/while
  1522.4 11.9 slice-start.4
  1541.0 8.7 copy-start.4
  1569.7 31.2 %slice-start = ((s8[15728640]{0:T(1024)(128)(4,1)}), s8[4194304]{0:T(1024)(128)(4,1)S(1)}, s32[]{:S(2)}) async-start(s8[15728640]{0:T(1024)(128)(4,1)} %bitcast.168), calls=%async_computation.8 | async-start | bytes 8388608 | tf_op jit(solution)/shard_map/while
  1569.7 31.2 %slice-start.1 = ((s8[15728640]{0:T(1024)(128)(4,1)}), s8[4194304]{0:T(1024)(128)(4,1)S(1)}, s32[]{:S(2)}) async-start(s8[15728640]{0:T(1024)(128)(4,1)} %bitcast.168), calls=%async_computation.9 | async-start | bytes 8388608 | tf_op jit(solution)/shard_map/while
  1569.7 31.2 %slice-start.2 = ((s8[15728640]{0:T(1024)(128)(4,1)}), s8[4194304]{0:T(1024)(128)(4,1)S(1)}, s32[]{:S(2)}) async-start(s8[15728640]{0:T(1024)(128)(4,1)} %bitcast.168), calls=%async_computation.10 | async-start | bytes 8388608 | tf_op jit(solution)/shard_map/while
  1569.8 31.2 %slice-start.3 = ((s8[15728640]{0:T(1024)(128)(4,1)}), s8[3145728]{0:T(1024)(128)(4,1)S(1)}, s32[]{:S(2)}) async-start(s8[15728640]{0:T(1024)(128)(4,1)} %bitcast.168), calls=%async_computation.11 | async-start | bytes 6291456 | tf_op jit(solution)/shard_map/while
  1595.1 11.9 slice-start.4
  1613.7 8.7 copy-start.4
  1642.5 31.2 %slice-start = ((s8[15728640]{0:T(1024)(128)(4,1)}), s8[4194304]{0:T(1024)(128)(4,1)S(1)}, s32[]{:S(2)}) async-start(s8[15728640]{0:T(1024)(128)(4,1)} %bitcast.168), calls=%async_computation.8 | async-start | bytes 8388608 | tf_op jit(solution)/shard_map/while
  1642.5 31.2 %slice-start.1 = ((s8[15728640]{0:T(1024)(128)(4,1)}), s8[4194304]{0:T(1024)(128)(4,1)S(1)}, s32[]{:S(2)}) async-start(s8[15728640]{0:T(1024)(128)(4,1)} %bitcast.168), calls=%async_computation.9 | async-start | bytes 8388608 | tf_op jit(solution)/shard_map/while
  1642.5 31.2 %slice-start.2 = ((s8[15728640]{0:T(1024)(128)(4,1)}), s8[4194304]{0:T(1024)(128)(4,1)S(1)}, s32[]{:S(2)}) async-start(s8[15728640]{0:T(1024)(128)(4,1)} %bitcast.168), calls=%async_computation.10 | async-start | bytes 8388608 | tf_op jit(solution)/shard_map/while
  1642.5 31.2 %slice-start.3 = ((s8[15728640]{0:T(1024)(128)(4,1)}), s8[3145728]{0:T(1024)(128)(4,1)S(1)}, s32[]{:S(2)}) async-start(s8[15728640]{0:T(1024)(128)(4,1)} %bitcast.168), calls=%async_computation.11 | async-start | bytes 6291456 | tf_op jit(solution)/shard_map/while
  1667.9 11.9 slice-start.4
  1686.5 8.7 copy-start.4
  1715.2 31.2 %slice-start = ((s8[15728640]{0:T(1024)(128)(4,1)}), s8[4194304]{0:T(1024)(128)(4,1)S(1)}, s32[]{:S(2)}) async-start(s8[15728640]{0:T(1024)(128)(4,1)} %bitcast.168), calls=%async_computation.8 | async-start | bytes 8388608 | tf_op jit(solution)/shard_map/while
  1715.2 31.2 %slice-start.1 = ((s8[15728640]{0:T(1024)(128)(4,1)}), s8[4194304]{0:T(1024)(128)(4,1)S(1)}, s32[]{:S(2)}) async-start(s8[15728640]{0:T(1024)(128)(4,1)} %bitcast.168), calls=%async_computation.9 | async-start | bytes 8388608 | tf_op jit(solution)/shard_map/while
  1715.2 31.2 %slice-start.2 = ((s8[15728640]{0:T(1024)(128)(4,1)}), s8[4194304]{0:T(1024)(128)(4,1)S(1)}, s32[]{:S(2)}) async-start(s8[15728640]{0:T(1024)(128)(4,1)} %bitcast.168), calls=%async_computation.10 | async-start | bytes 8388608 | tf_op jit(solution)/shard_map/while
  1715.2 31.2 %slice-start.3 = ((s8[15728640]{0:T(1024)(128)(4,1)}), s8[3145728]{0:T(1024)(128)(4,1)S(1)}, s32[]{:S(2)}) async-start(s8[15728640]{0:T(1024)(128)(4,1)} %bitcast.168), calls=%async_computation.11 | async-start | bytes 6291456 | tf_op jit(solution)/shard_map/while
  1740.6 11.9 slice-start.4
  1768.4 664.7 %reduce-scatter.2.cloned.1.call-start = ((), (), s32[]{:S(2)}) async-start(), calls=%async_computation.6 | async-start | bytes 10616832 | tf_op jit(solution)/shard_map/reduce_scatter | solution.py:357
  1897.1 50.0 %slice-start.6 = ((s8[7864320]{0:T(1024)(128)(4,1)}), s8[4194304]{0:T(1024)(128)(4,1)S(1)}, s32[]{:S(2)}) async-start(s8[7864320]{0:T(1024)(128)(4,1)} %bitcast.174), calls=%async_computation.14 | async-start | bytes 8388608
  1904.0 37.4 %copy-start.6 = (bf16[2560,768]{1,0:T(8,128)(2,1)S(1)}, bf16[2560,768]{1,0:T(8,128)(2,1)}, u32[]{:S(2)}) copy-start(bf16[2560,768]{1,0:T(8,128)(2,1)} %param.20) | copy-start | bytes 11796484
  1904.0 37.4 %copy-start.27 = (f32[2560]{0:T(1024)S(1)}, f32[2560]{0:T(1024)}, u32[]{:S(2)}) copy-start(f32[2560]{0:T(1024)} %copy-done.26) | copy-start | bytes 30724
  1904.0 37.4 %copy-start.35 = (f32[768]{0:T(1024)S(1)}, f32[768]{0:T(1024)}, u32[]{:S(2)}) copy-start(f32[768]{0:T(1024)} %copy-done.34) | copy-start | bytes 9220
  1904.0 43.1 %slice-start.7 = ((s8[7864320]{0:T(1024)(128)(4,1)}), s8[3670016]{0:T(1024)(128)(4,1)S(1)}, s32[]{:S(2)}) async-start(s8[7864320]{0:T(1024)(128)(4,1)} %bitcast.174), calls=%async_computation.15 | async-start | bytes 7340032
  1973.0 21.8 copy-start.38
  2376.4 7.4 copy-start.43
  2428.7 7.3 copy-start.32
  2428.7 7.3 copy-start.40
  2435.9 52.4 %copy-start.14 = (f32[2,192,768]{2,1,0:T(8,128)S(1)}, f32[2,192,768]{2,1,0:T(8,128)}, u32[]{:S(2)}) copy-start(f32[2,192,768]{2,1,0:T(8,128)} %param.24) | copy-start | bytes 3538948
  2436.0 52.4 %copy-start.15 = (f32[2,192,768]{2,1,0:T(8,128)S(1)}, f32[2,192,768]{2,1,0:T(8,128)}, u32[]{:S(2)}) copy-start(f32[2,192,768]{2,1,0:T(8,128)} %reduce-scatter.2.cloned.1.call-done) | copy-start | bytes 3538948
  2436.0 52.3 %copy-start.17 = (f32[2,192,768]{2,1,0:T(8,128)S(1)}, f32[2,192,768]{2,1,0:T(8,128)}, u32[]{:S(2)}) copy-start(f32[2,192,768]{2,1,0:T(8,128)} %param.26) | copy-start | bytes 3538948
  (29 other events, 117.7 us)
Sparse Core Ops, SparseCore 0:
  10.8 82.5 all-gather.3
  754.1 147.9 all-reduce.13
  921.2 145.3 all-reduce.15
  1118.5 69.5 all-reduce.21
  1228.6 144.3 all-reduce.17
  1768.5 145.4 all-reduce.19
  1973.1 163.7 reduce-scatter.1
where the time goes:
time: 2550 us; the launch traced here: 2500 us
  local copies, waits for them, and re-layouts  1230 us (48%)
  waiting for transfers between devices  489 us (19%)
  matrix products  346 us (14%)
  other arithmetic  268 us (11%)
  blocking collectives  121 us (5%)
  between operations  28.6 us (1%)
    unnamed x129, local copies, waits for them, and re-layouts  847 us
    psum x1, waiting for transfers between devices, on_device(): attn_total = lax.psum(plain_product(context, out_weight), 'narrow')  146 us
    psum x1, waiting for transfers between devices, on_device(): ffn_total = lax.psum(plain_product(hidden_low, outer_weight), 'narrow')  145 us
    dot_general x10, matrix products, block_scores(): jnp.einsum('qhd,khd->hqk', query_block, key_block, preferred_element_type...  140 us
    psum x1, waiting for transfers between devices, on_device(): normed_two_grad = lax.psum(plain_product(pre_low, inner_weight), 'narrow')  130 us
    add x5, other arithmetic, backward_block(): score_acc = score_acc + score_grad.astype(jnp.float32)  122 us
    rev x1, local copies, waits for them, and re-layouts, diagonal_sums(): flipped = blocks[:, ::-1, :]  120 us
    rev x1, local copies, waits for them, and re-layouts, toeplitz_rows(): return shaped[:, ::-1, :]  120 us
  transfers between devices with their start and end apart: 7, of which 4 were waited for; matrix products, arithmetic and copies ran while one was open for 48% of the time, Pallas kernels for 0%

commit v1 on v0

--- a/solution.py
+++ b/solution.py
@@ -1,6 +1,8 @@
 import jax
 import jax.numpy as jnp
 from jax import lax
+from jax.experimental import pallas as pl
+from jax.experimental.pallas import tpu as pltpu
 from jax.sharding import PartitionSpec as P
 
 D = 768
@@ -9,9 +11,16 @@
 TOK_DEV = 2560
 SEQS_DEV = 4
 DOCLEN = 1024
-QBLOCK = 512
 CAP = 2
 STEP = 10
+LANE = 128
+BQ = 512
+BK = 512
+REACH = DOCLEN // LANE
+OFF = REACH + (BQ + BK) // LANE
+SPAN = 2 * OFF + 1
+LINES = 2 * REACH + 2
+VMEM_LIMIT = 56 * 1024 * 1024
 
 
 norm_eps = 1e-06
@@ -54,25 +63,176 @@
     return (value_grad, gain_grad)
 
 
-def toeplitz_rows(extended, row_count, column_count):
-    head_count = extended.shape[0]
-    full_length = extended.shape[1]
-    repeated = jnp.broadcast_to(extended[:, None, :], (head_count, row_count, full_length)).reshape(
-        head_count, row_count * full_length
-    )
-    padded = jnp.pad(repeated, ((0, 0), (0, row_count)))
-    shaped = padded.reshape(head_count, row_count, full_length + 1)[:, :, :column_count]
-    return shaped[:, ::-1, :]
-
-
-def diagonal_sums(blocks, row_count, column_count):
-    head_count = blocks.shape[0]
-    flipped = blocks[:, ::-1, :]
-    padded = jnp.pad(flipped, ((0, 0), (0, 0), (0, row_count)))
-    flattened = padded.reshape(head_count, row_count * (column_count + row_count))
-    flattened = flattened[:, : row_count * (column_count + row_count - 1)]
-    skewed = flattened.reshape(head_count, row_count, column_count + row_count - 1)
-    return jnp.sum(skewed, axis=1)
+def nn(a,b): return lax.dot_general(a,b,(((1,),(0,)),((),())),preferred_element_type=jnp.float32)
+def nt(a,b): return lax.dot_general(a,b,(((1,),(1,)),((),())),preferred_element_type=jnp.float32)
+
+def bias_kernel(chunks, tiles):
+    heads=tiles.shape[0]
+    tiles[...]=jnp.zeros_like(tiles)
+    for h in range(heads):
+        for d in range(-REACH,REACH+1):
+            left=chunks[h,REACH+1-d:REACH+2-d,:]
+            right=chunks[h,REACH-d:REACH+1-d,:]
+            line=jnp.concatenate([left,right],axis=1)
+            rolled=pltpu.roll(jnp.broadcast_to(line,(LANE,2*LANE)),0,1,stride=1,stride_axis=0)
+            tiles[h,pl.ds((d+OFF)*LANE,LANE),:]=rolled[:,:LANE]
+
+def bias_tiles(rel_chunks):
+    heads=rel_chunks.shape[0]
+    return pl.pallas_call(bias_kernel,
+        out_shape=jax.ShapeDtypeStruct((heads,SPAN*LANE,LANE),jnp.float32),
+        compiler_params=pltpu.CompilerParams(vmem_limit_bytes=VMEM_LIMIT),
+        name="bias_tiles")(rel_chunks)
+
+def key_range(lengths, first, last):
+    start=jnp.int32(0); end=jnp.int32(0); low=jnp.int32(0); high=jnp.int32(0)
+    found=jnp.int32(0)
+    for s in range(lengths.shape[0]):
+        end=start+lengths[s]
+        low=jnp.where(start<=first,start,low)
+        high=jnp.where(start<=last,end,high)
+        start=end
+    return low//BK,(high+BK-1)//BK
+
+def bias_part(bias,h,i,j):
+    row=(j*(BK//LANE)-i*(BQ//LANE)+OFF)*LANE
+    return jnp.concatenate([bias[h,pl.ds(pl.multiple_of(row-b*LANE,LANE),BK),:] for b in range(BQ//LANE)],axis=1)
+
+def forward_kernel(lengths,qT,kn,vT,exq,bias,ctx_o,ctxT_o,lse_o,qa,acc):
+    tokens=qT.shape[1]
+    heads=bias.shape[0]
+    hs=qT.shape[0]//heads
+    qa[...]=jnp.zeros_like(qa)
+    @pl.loop(0,tokens//BQ)
+    def _(i):
+        q0=pl.multiple_of(i*BQ,BQ)
+        for h in range(heads):
+            qa[h*LANE:h*LANE+hs,:]=qT[h*hs:(h+1)*hs,pl.ds(q0,BQ)]
+            qa[h*LANE+hs:h*LANE+hs+16,:]=exq[:,pl.ds(q0,BQ)]
+        acc[...]=jnp.zeros_like(acc)
+        low,high=key_range(lengths,q0,q0+BQ-1)
+        def step(j,carry):
+            k0=pl.multiple_of(j*BK,BK)
+            out=[]
+            for h in range(heads):
+                top,total=carry[2*h],carry[2*h+1]
+                s=nn(kn[pl.ds(k0,BK),h*LANE:(h+1)*LANE],qa[h*LANE:(h+1)*LANE,:])
+                s=s+bias_part(bias,h,i,j)
+                new_top=jnp.maximum(top,jnp.max(s,axis=0,keepdims=True))
+                fade=jnp.exp(top-new_top)
+                p=jnp.exp(s-new_top)
+                total=total*fade+jnp.sum(p,axis=0,keepdims=True)
+                rows=slice(h*hs,(h+1)*hs)
+                acc[rows,:]=acc[rows,:]*fade+nn(vT[rows,pl.ds(k0,BK)],p.astype(jnp.bfloat16))
+                out+=[new_top,total]
+            return tuple(out)
+        init=tuple(jnp.full((1,BQ),2.0*masked_score if n%2==0 else 0.0,jnp.float32) for n in range(2*heads))
+        done=lax.fori_loop(low,high,step,init)
+        lse=[]
+        for h in range(heads):
+            rows=slice(h*hs,(h+1)*hs)
+            acc[rows,:]=acc[rows,:]/done[2*h+1]
+            lse_o[h:h+1,pl.ds(q0,BQ)]=done[2*h]+jnp.log(done[2*h+1])
+        ctxT_o[:,pl.ds(q0,BQ)]=acc[...]
+        ctx_o[pl.ds(q0,BQ),:]=acc[...].T.astype(jnp.bfloat16)
+
+def smem(): return pl.BlockSpec(memory_space=pltpu.SMEM)
+def vmem(): return pl.BlockSpec(memory_space=pltpu.VMEM)
+
+def attention_forward(lengths,qT,kn,vT,exq,bias):
+    width,tokens=qT.shape
+    heads=bias.shape[0]
+    return pl.pallas_call(forward_kernel,
+        out_shape=(jax.ShapeDtypeStruct((tokens,width),jnp.bfloat16),jax.ShapeDtypeStruct((width,tokens),jnp.float32),jax.ShapeDtypeStruct((heads,tokens),jnp.float32)),
+        in_specs=[smem()]+[vmem()]*5, out_specs=(vmem(),)*3,
+        scratch_shapes=[pltpu.VMEM((heads*LANE,BQ),jnp.bfloat16),pltpu.VMEM((width,BQ),jnp.float32)],
+        compiler_params=pltpu.CompilerParams(vmem_limit_bytes=VMEM_LIMIT),
+        name="attention_forward")(lengths,qT,kn,vT,exq,bias)
+
+def split3(v):
+    a=v.astype(jnp.bfloat16); r=v-a.astype(jnp.float32)
+    b=r.astype(jnp.bfloat16); c=r-b.astype(jnp.float32)
+    return a.astype(jnp.float32),b.astype(jnp.float32),c
+
+def backward_kernel(lengths,qT,kn,vn,kT,dcT,ctxT,lse,exq,bias,dT_o,dn_o,lines_o,qa,da,dq,dk,dv,tiles):
+    width,tokens=qT.shape
+    heads=bias.shape[0]
+    hs=width//heads
+    qa[...]=jnp.zeros_like(qa)
+    da[...]=jnp.zeros_like(da)
+    dk[...]=jnp.zeros_like(dk)
+    dv[...]=jnp.zeros_like(dv)
+    tiles[...]=jnp.zeros_like(tiles)
+    place=lax.broadcasted_iota(jnp.int32,(16,BQ),0)
+    def pieces(v):
+        a,b,c=split3(v)
+        return jnp.where(place==4,a,jnp.where(place==5,b,jnp.where(place==6,c,0.0)))
+    @pl.loop(0,tokens//BQ)
+    def _(i):
+        q0=pl.multiple_of(i*BQ,BQ)
+        for h in range(heads):
+            rows=slice(h*hs,(h+1)*hs)
+            qa[h*LANE:h*LANE+hs,:]=qT[rows,pl.ds(q0,BQ)]
+            qa[h*LANE+hs:h*LANE+hs+16,:]=(exq[:,pl.ds(q0,BQ)].astype(jnp.float32)+pieces(-lse[h:h+1,pl.ds(q0,BQ)])).astype(jnp.bfloat16)
+            dc=dcT[rows,pl.ds(q0,BQ)]
+            delta=jnp.sum(dc.astype(jnp.float32)*ctxT[rows,pl.ds(q0,BQ)],axis=0,keepdims=True)
+            da[h*LANE:h*LANE+hs,:]=dc
+            da[h*LANE+hs:h*LANE+hs+16,:]=pieces(-delta).astype(jnp.bfloat16)
+        dq[...]=jnp.zeros_like(dq)
+        low,high=key_range(lengths,q0,q0+BQ-1)
+        @pl.loop(low,high)
+        def _(j):
+            k0=pl.multiple_of(j*BK,BK)
+            base=(j*(BK//LANE)-i*(BQ//LANE)+OFF)*LANE
+            for h in range(heads):
+                rows=slice(h*hs,(h+1)*hs)
+                own=slice(h*LANE,(h+1)*LANE)
+                s=nn(kn[pl.ds(k0,BK),own],qa[own,:])
+                p=jnp.exp(s+bias_part(bias,h,i,j))
+                dp=nn(vn[pl.ds(k0,BK),own],da[own,:])
+                ds=p*dp
+                for b in range(BQ//LANE):
+                    at=pl.ds(pl.multiple_of(base-b*LANE,LANE),BK)
+                    tiles[h,at,:]=tiles[h,at,:]+ds[:,b*LANE:(b+1)*LANE]
+                pb=p.astype(jnp.bfloat16)
+                db=ds.astype(jnp.bfloat16)
+                dv[rows,pl.ds(k0,BK)]=dv[rows,pl.ds(k0,BK)]+nt(da[h*LANE:h*LANE+hs,:],pb)
+                dk[rows,pl.ds(k0,BK)]=dk[rows,pl.ds(k0,BK)]+nt(qa[h*LANE:h*LANE+hs,:],db)
+                dq[rows,:]=dq[rows,:]+nn(kT[rows,pl.ds(k0,BK)],db)
+        grad=dq[...]*0.125
+        dT_o[0:width,pl.ds(q0,BQ)]=grad.astype(jnp.bfloat16)
+        dn_o[pl.ds(q0,BQ),0:width]=grad.T.astype(jnp.bfloat16)
+    @pl.loop(0,tokens//BQ)
+    def _(i):
+        q0=pl.multiple_of(i*BQ,BQ)
+        both=jnp.concatenate([dk[:,pl.ds(q0,BQ)],dv[:,pl.ds(q0,BQ)]],axis=0)
+        dT_o[width:3*width,pl.ds(q0,BQ)]=both.astype(jnp.bfloat16)
+        dn_o[pl.ds(q0,BQ),width:3*width]=both.T.astype(jnp.bfloat16)
+    over=lax.broadcasted_iota(jnp.int32,(LANE,LANE),1)>=lax.broadcasted_iota(jnp.int32,(LANE,LANE),0)
+    sub=lax.broadcasted_iota(jnp.int32,(8,LANE),0)
+    for h in range(heads):
+        for d in range(-REACH,REACH+2):
+            here=tiles[h,(d+OFF)*LANE:(d+OFF+1)*LANE,:]
+            below=tiles[h,(d+OFF-1)*LANE:(d+OFF)*LANE,:]
+            mixed=jnp.where(over,here,below)
+            line=mixed[LANE-8:,:]
+            for g in range(LANE//8-2,-1,-1):
+                line=mixed[8*g:8*g+8,:]+pltpu.roll(line,LANE-8,1)
+            for bit in (1,2,4):
+                line=jnp.where((sub&bit)!=0,pltpu.roll(line,LANE-bit,1),line)
+            lines_o[h,REACH+1-d:REACH+2-d,:]=jnp.sum(line,axis=0,keepdims=True)
+
+def attention_backward(lengths,qT,kn,vn,kT,dcT,ctxT,lse,exq,bias):
+    width,tokens=qT.shape
+    heads=bias.shape[0]
+    return pl.pallas_call(backward_kernel,
+        out_shape=(jax.ShapeDtypeStruct((3*width,tokens),jnp.bfloat16),jax.ShapeDtypeStruct((tokens,3*width),jnp.bfloat16),jax.ShapeDtypeStruct((heads,2*REACH+2,LANE),jnp.float32)),
+        in_specs=[smem()]+[vmem()]*9, out_specs=(vmem(),)*3,
+        scratch_shapes=[pltpu.VMEM((heads*LANE,BQ),jnp.bfloat16),pltpu.VMEM((heads*LANE,BQ),jnp.bfloat16),
+            pltpu.VMEM((width,BQ),jnp.float32),pltpu.VMEM((width,tokens),jnp.float32),pltpu.VMEM((width,tokens),jnp.float32),
+            pltpu.VMEM((heads,SPAN*LANE,LANE),jnp.float32)],
+        compiler_params=pltpu.CompilerParams(vmem_limit_bytes=VMEM_LIMIT),
+        name="attention_backward")(lengths,qT,kn,vn,kT,dcT,ctxT,lse,exq,bias)
 
 
 def decoupled_decay_step(gradient, first_moment, second_moment, weight, multiplier, step_rate):
@@ -112,8 +272,6 @@
     heads_here = distance_bias_table.shape[1]
     head_size = unit_rows // heads_here
     ffn_units = FF // D
-    window = QBLOCK + 2 * DOCLEN
-    block_count = TOK_DEV // QBLOCK
     every_slot = lax.all_gather(
         precise_parameter_blocks.astype(jnp.bfloat16), "wide", axis=0, tiled=True
     ).astype(precise_parameter_blocks.dtype)
@@ -129,56 +287,40 @@
     seq_ends = jnp.cumsum(lengths)
     positions = jnp.arange(TOK_DEV, dtype=jnp.int32)
     segment_ids = jnp.sum((seq_ends[None, :] <= positions[:, None]).astype(jnp.int32), axis=1)
-    segment_padded = jnp.pad(segment_ids, (DOCLEN, DOCLEN), constant_values=-1)
+    beyond = LINES * LANE - LANE - 1 - distance_bin_lookup.shape[0]
+    offsets_down = jnp.pad(distance_bin_lookup[::-1], (LANE + 1, beyond), constant_values=-1)
     bucket_onehot = (
-        distance_bin_lookup[:, None] == jnp.arange(BUCKETS, dtype=jnp.int32)[None, :]
+        offsets_down[:, None] == jnp.arange(BUCKETS, dtype=jnp.int32)[None, :]
     ).astype(jnp.float32)
     rel_values = jnp.dot(bucket_onehot, distance_bias_table, precision=lax.Precision.HIGHEST).T
-    bias_block = toeplitz_rows(jnp.pad(rel_values, ((0, 0), (QBLOCK, QBLOCK))), QBLOCK, window)
+    tiles_bias = bias_tiles(rel_values.reshape(heads_here, LINES, LANE))
     scale_one = rms_scale(arguments_list)
     normed_one = (arguments_list * scale_one * rescaling_coefficients[0]).astype(jnp.bfloat16)
-    projections = times_transposed(normed_one, qkv_weight).astype(jnp.bfloat16)
-    query_rows = projections[:, :unit_rows]
-    key_padded = jnp.pad(projections[:, unit_rows : 2 * unit_rows], ((DOCLEN, DOCLEN), (0, 0)))
-    value_padded = jnp.pad(projections[:, 2 * unit_rows :], ((DOCLEN, DOCLEN), (0, 0)))
-
-    def block_scores(block_start):
-        query_block = lax.dynamic_slice_in_dim(query_rows, block_start, QBLOCK, 0).reshape(
-            QBLOCK, heads_here, head_size
-        )
-        key_block = lax.dynamic_slice_in_dim(key_padded, block_start, window, 0).reshape(
-            window, heads_here, head_size
-        )
-        value_block = lax.dynamic_slice_in_dim(value_padded, block_start, window, 0).reshape(
-            window, heads_here, head_size
-        )
-        scores = (
-            jnp.einsum("qhd,khd->hqk", query_block, key_block, preferred_element_type=jnp.float32)
-            * score_scale
-            + bias_block
-        )
-        query_segments = lax.dynamic_slice_in_dim(segment_ids, block_start, QBLOCK, 0)
-        key_segments = lax.dynamic_slice_in_dim(segment_padded, block_start, window, 0)
-        allowed = query_segments[:, None] == key_segments[None, :]
-        scores = jnp.where(allowed[None, :, :], scores, masked_score)
-        return (scores, query_block, key_block, value_block)
-
-    def forward_block(state_in, block_index):
-        block_start = block_index * QBLOCK
-        scores, query_block, key_block, value_block = block_scores(block_start)
-        row_top = jnp.max(scores, axis=-1, keepdims=True)
-        weights = jnp.exp(scores - row_top)
-        row_total = jnp.sum(weights, axis=-1, keepdims=True)
-        probabilities = (weights / row_total).astype(jnp.bfloat16)
-        context_block = jnp.einsum(
-            "hqk,khd->qhd", probabilities, value_block, preferred_element_type=jnp.float32
-        )
-        return (state_in, (context_block.reshape(QBLOCK, unit_rows), row_top + jnp.log(row_total)))
-
-    state_out, (context_blocks, log_blocks) = lax.scan(
-        forward_block, jnp.zeros((), jnp.float32), jnp.arange(block_count, dtype=jnp.int32)
-    )
-    context = context_blocks.reshape(TOK_DEV, unit_rows).astype(jnp.bfloat16)
+    transposed_rows = times_transposed(qkv_weight, normed_one)
+    query_cols = (transposed_rows[:unit_rows] * score_scale).astype(jnp.bfloat16)
+    key_cols = transposed_rows[unit_rows : 2 * unit_rows].astype(jnp.bfloat16)
+    value_cols = transposed_rows[2 * unit_rows :].astype(jnp.bfloat16)
+    spread_weight = jnp.pad(
+        weights_low[1:3].reshape(2 * heads_here, head_size, D),
+        ((0, 0), (0, LANE - head_size), (0, 0)),
+    ).reshape(2 * heads_here * LANE, D)
+    lane_place = jnp.arange(2 * heads_here * LANE, dtype=jnp.int32) % LANE - head_size
+    marks = jnp.logical_or(
+        lane_place[None, :] == segment_ids[:, None],
+        jnp.logical_and(lane_place >= SEQS_DEV, lane_place < SEQS_DEV + 3)[None, :],
+    )
+    key_value_rows = (
+        times_transposed(normed_one, spread_weight) + marks.astype(jnp.float32)
+    ).astype(jnp.bfloat16)
+    key_rows = key_value_rows[:, : heads_here * LANE]
+    value_rows = key_value_rows[:, heads_here * LANE :]
+    row_place = jnp.arange(16, dtype=jnp.int32)[:, None]
+    apart = jnp.where(
+        jnp.logical_and(row_place < SEQS_DEV, row_place != segment_ids[None, :]), masked_score, 0.0
+    ).astype(jnp.bfloat16)
+    context, context_cols, log_rows = attention_forward(
+        lengths, query_cols, key_rows, value_cols, apart, tiles_bias
+    )
     attn_total = lax.psum(plain_product(context, out_weight), "narrow")
     residual_mid = arguments_list + attn_total
     scale_two = rms_scale(residual_mid)
@@ -262,69 +404,29 @@
     )
     mid_grad = encoded_grad + mid_norm_grad
     attn_grad_low = mid_grad.astype(jnp.bfloat16)
-    context_grad = times_transposed(attn_grad_low, out_weight).astype(jnp.bfloat16)
+    context_grad = times_transposed(out_weight, attn_grad_low).astype(jnp.bfloat16)
     out_grad = outer_product(context, attn_grad_low)
 
-    def backward_block(state_in, block_index):
-        key_acc, value_acc, score_acc = state_in
-        block_start = block_index * QBLOCK
-        scores, query_block, key_block, value_block = block_scores(block_start)
-        probabilities = jnp.exp(scores - log_blocks[block_index])
-        context_block = lax.dynamic_slice_in_dim(context_grad, block_start, QBLOCK, 0).reshape(
-            QBLOCK, heads_here, head_size
-        )
-        prob_grad = jnp.einsum(
-            "qhd,khd->hqk", context_block, value_block, preferred_element_type=jnp.float32
-        )
-        row_delta = jnp.sum(probabilities * prob_grad, axis=-1, keepdims=True)
-        score_grad = (probabilities * (prob_grad - row_delta)).astype(jnp.bfloat16)
-        value_part = jnp.einsum(
-            "hqk,qhd->khd",
-            probabilities.astype(jnp.bfloat16),
-            context_block,
-            preferred_element_type=jnp.float32,
-        )
-        query_part = (
-            jnp.einsum("hqk,khd->qhd", score_grad, key_block, preferred_element_type=jnp.float32)
-            * score_scale
-        )
-        key_part = (
-            jnp.einsum("hqk,qhd->khd", score_grad, query_block, preferred_element_type=jnp.float32)
-            * score_scale
-        )
-        key_old = lax.dynamic_slice_in_dim(key_acc, block_start, window, 0)
-        key_acc = lax.dynamic_update_slice_in_dim(
-            key_acc, key_old + key_part.reshape(window, unit_rows), block_start, 0
-        )
-        value_old = lax.dynamic_slice_in_dim(value_acc, block_start, window, 0)
-        value_acc = lax.dynamic_update_slice_in_dim(
-            value_acc, value_old + value_part.reshape(window, unit_rows), block_start, 0
-        )
-        score_acc = score_acc + score_grad.astype(jnp.float32)
-        return ((key_acc, value_acc, score_acc), query_part.reshape(QBLOCK, unit_rows))
-
-    empty_rows = jnp.zeros((TOK_DEV + 2 * DOCLEN, unit_rows), jnp.float32)
-    empty_scores = jnp.zeros((heads_here, QBLOCK, window), jnp.float32)
-    (key_acc, value_acc, score_acc), query_blocks = lax.scan(
-        backward_block,
-        (empty_rows, empty_rows, empty_scores),
-        jnp.arange(block_count, dtype=jnp.int32),
-    )
-    qkv_low = jnp.concatenate(
-        [
-            query_blocks.reshape(TOK_DEV, unit_rows),
-            key_acc[DOCLEN : DOCLEN + TOK_DEV],
-            value_acc[DOCLEN : DOCLEN + TOK_DEV],
-        ],
-        axis=1,
-    ).astype(jnp.bfloat16)
-    diagonals = diagonal_sums(score_acc, QBLOCK, window)
-    rel_grad = diagonals[:, QBLOCK : QBLOCK + 2 * DOCLEN - 1]
+    qkv_cols, qkv_rows, bias_lines = attention_backward(
+        lengths,
+        query_cols,
+        key_rows,
+        value_rows,
+        key_cols,
+        context_grad,
+        context_cols,
+        log_rows,
+        apart,
+        tiles_bias,
+    )
     offset_bias_slope = lax.dot_general(
-        bucket_onehot, rel_grad, (((0,), (1,)), ((), ())), precision=lax.Precision.HIGHEST
-    )
-    qkv_weight_grad = outer_product(qkv_low, normed_one)
-    normed_one_grad = lax.psum(plain_product(qkv_low, qkv_weight), "narrow")
+        bucket_onehot,
+        bias_lines.reshape(heads_here, LINES * LANE),
+        (((0,), (1,)), ((), ())),
+        precision=lax.Precision.HIGHEST,
+    )
+    qkv_weight_grad = plain_product(qkv_cols, normed_one)
+    normed_one_grad = lax.psum(plain_product(qkv_rows, qkv_weight), "narrow")
     input_norm_grad, attn_gain_grad = norm_backward(
         arguments_list, scale_one, rescaling_coefficients[0], normed_one_grad
     )

time: 2550 us -> 1240 us (0.49); the launches traced: 2500 us -> 1220 us
  local copies, waits for them, and re-layouts: 1230 us -> 50.1 us
  waiting for transfers between devices: 489 us -> 794 us
  matrix products: 346 us -> 88.7 us
  other arithmetic: 268 us -> 70.1 us
  Pallas kernels: 0 us -> 64.6 us
    unnamed x129 -> x80, local copies, waits for them, and re-layouts: 847 us -> 16.9 us
    dot_general x36 -> x1, matrix products: 263 us -> 0.62 us  [on_device(): lax.dot_general(bucket_onehot, bias_lines.reshape(heads_here, LINES * LAN...]
    rev x2 -> x0, local copies, waits for them, and re-layouts: 240 us -> none  [the longest x1 120 us: diagonal_sums(): flipped = blocks[:, ::-1, :]]
    add x5 -> x0, other arithmetic: 122 us -> none  [backward_block(): score_acc = score_acc + score_grad.astype(jnp.float32)]
    reduce_scatter x1, waiting for transfers between devices: 0.01 us -> 117 us  [on_device(): lax.psum_scatter(placed, 'wide', scatter_dimension=0, tiled=True)]
    psum x1, waiting for transfers between devices: 0.02 us -> 101 us  [on_device(): normed_one_grad = lax.psum(plain_product(qkv_rows, qkv_weight), 'narrow')]
    all_gather x1, waiting for transfers between devices: 0.02 us -> 70.5 us  [on_device(): lax.all_gather(precise_parameter_blocks.astype(jnp.bfloat16), 'wide', axi...]
    pallas_call x0 -> x3, Pallas kernels: none -> 64.6 us  [the longest x1 34.8 us: attention_backward(): pl.pallas_call(backward_kernel, out_shape=(jax.ShapeDtypeStruct((3 * widt...]
  transfers between devices with their start and end apart: 7 -> 7, of which waited for: 4 -> 7; matrix products, arithmetic and copies ran while one was open for 48% -> 5% of each run, Pallas kernels for 0% -> 0%
where the time goes in v1:
time: 1240 us; the launch traced here: 1220 us
  waiting for transfers between devices  794 us (64%)
  blocking collectives  126 us (10%)
  matrix products  88.7 us (7%)
  other arithmetic  70.1 us (6%)
  Pallas kernels  64.6 us (5%)
  local copies, waits for them, and re-layouts  50.1 us (4%)
  between operations  28.4 us (2%)
    psum x1, waiting for transfers between devices, on_device(): attn_total = lax.psum(plain_product(context, out_weight), 'narrow')  148 us
    psum x1, waiting for transfers between devices, on_device(): ffn_total = lax.psum(plain_product(hidden_low, outer_weight), 'narrow')  145 us
    psum x1, waiting for transfers between devices, on_device(): normed_two_grad = lax.psum(plain_product(pre_low, inner_weight), 'narrow')  144 us
    reduce_scatter x1, waiting for transfers between devices, on_device(): lax.psum_scatter(placed, 'wide', scatter_dimension=0, tiled=True)  117 us
    psum x1, waiting for transfers between devices, on_device(): normed_one_grad = lax.psum(plain_product(qkv_rows, qkv_weight), 'narrow')  101 us
    all_gather x1, waiting for transfers between devices, on_device(): lax.all_gather(precise_parameter_blocks.astype(jnp.bfloat16), 'wide', axi...  70.5 us
    unnamed x8, waiting for transfers between devices  68.5 us
    psum x1, blocking collectives, on_device(): lax.psum((norm_scale_slopes, offset_bias_slope, sharpness_derivative.resh...  40.2 us
  transfers between devices with their start and end apart: 7, of which 7 were waited for; matrix products, arithmetic and copies ran while one was open for 5% of the time, Pallas kernels for 0%

profile of v1, /device:TPU:0, one launch (start us, length us, event | category | flops | bytes accessed | tf_op | source)
XLA Modules:
  0.0 1222.4 jit_solution(18380590520012504432)
XLA Ops:
  7.3 2.1 convert_element_type.87
  10.4 2.3 convolution_bitcast_fusion
  13.3 5.3 bias_tiles.1.bias
  19.1 3.1 fusion.14
  23.0 70.5 %all-gather.4.cloned.1.call-done = bf16[16,192,768]{2,1,0:T(8,128)(2,1)} async-done(((bf16[2,192,768]{2,1,0:T(8,128)(2,1)}), bf16[16,192,768]{2,1,0:T(8,128)(2,1)}) %all-gather.4.cloned.1.call-update) | async-done | bytes 4718608 | tf_op jit(solution)/shard_map/all_gather | solution.py:275
  93.4 5.1 gather_fusion
  98.5 3.2 select_convert_fusion
  102.0 4.7 add_convert_fusion
  106.7 2.3 fusion.92
  109.0 2.6 fusion.95
  111.6 1.4 fusion.94
  113.0 1.1 fusion.23.qT
  114.1 24.4 %attention_forward.1 = (bf16[2560,192]{1,0:T(8,128)(2,1)}, f32[192,2560]{1,0:T(8,128)}, f32[3,2560]{1,0:T(4,128)}) custom-call(s32[4]{0:T(128)} %bitcast.92, bf16[192,2560]{1,0:T(8,128)(2,1)} %fusion.23.qT, bf16[2560,384]{1,0:T(8,128)(2,1)} %get-tuple-element.59.kn, bf16[192,2560]{1,0:T(8,128)(2,1)} %get-tuple-element.63.vT, ...), custom_call_target="tpu_custom_call" | custom-call | tf_op jit(solution)/shard_map/attention_forward/pallas_call | solution.py:145
  138.5 5.7 fusion.52
  144.5 1.8 fusion.93
  146.3 147.7 %all-reduce.10.cloned.1.call-done = f32[2560,768]{1,0:T(8,128)} async-done(((f32[2560,768]{1,0:T(8,128)}), f32[2560,768]{1,0:T(8,128)}) %all-reduce.10.cloned.1.call-update) | async-done | bytes 7864336 | tf_op jit(solution)/shard_map/psum | solution.py:324
  294.0 5.4 multiply_reduce_fusion.5
  299.5 3.4 fusion.82
  303.0 3.1 copy-done.32
  306.0 6.9 fusion.88
  313.7 144.8 %all-reduce.12.cloned.1.call-done = f32[2560,768]{1,0:T(8,128)} async-done(((f32[2560,768]{1,0:T(8,128)}), f32[2560,768]{1,0:T(8,128)}) %all-reduce.12.cloned.1.call-update) | async-done | bytes 7864336 | tf_op jit(solution)/shard_map/psum | solution.py:331
  458.5 6.4 multiply_reduce_fusion.4
  465.0 3.2 copy-done.1
  468.1 3.2 fusion.47
  471.4 1.1 fusion.43
  472.5 5.2 all-gather
  478.0 30.7 %all-gather.1 = bf16[8,4,768]{2,1,0:T(4,128)(2,1)S(1)} all-gather(bf16[1,4,768]{2,1,0:T(4,128)(2,1)S(1)} %get-tuple-element.52), channel_id=1, replica_groups=mesh['wide'=8,'narrow'=4] {'wide'}, dimensions={0}, use_global_device_ids=true | all-gather | bytes 55296 | tf_op jit(solution)/shard_map/all_gather | solution.py:345
  509.2 1.0 convolution_multiply_fusion
  511.5 68.4 %all-reduce.18.cloned.1.call-done = f32[32,768]{1,0:T(8,128)} async-done(((f32[32,768]{1,0:T(8,128)}), f32[32,768]{1,0:T(8,128)}) %all-reduce.18.cloned.1.call-update) | async-done | bytes 98320
  579.9 1.1 fusion.63
  581.1 1.1 fusion.53
  582.2 10.5 psum.73
  592.7 8.0 multiply_reduce_fusion
  600.7 4.5 multiply_subtract_fusion
  605.4 7.4 fusion.13
  612.9 1.9 copy-done.11
  614.8 5.3 fusion.96
  620.3 144.3 %all-reduce.14.cloned.1.call-done = f32[2560,768]{1,0:T(8,128)} async-done(((f32[2560,768]{1,0:T(8,128)}), f32[2560,768]{1,0:T(8,128)}) %all-reduce.14.cloned.1.call-update) | async-done | bytes 7864336 | tf_op jit(solution)/shard_map/psum | solution.py:401
  764.7 6.8 multiply_reduce_fusion.1
  772.4 6.9 subtract_add_fusion
  779.3 3.1 copy-done.2
  782.4 3.3 convolution_convert_fusion.dcT
  785.7 34.8 %attention_backward.1 = (bf16[576,2560]{1,0:T(8,128)(2,1)}, bf16[2560,576]{1,0:T(8,128)(2,1)}, f32[3,18,128]{2,1,0:T(8,128)}) custom-call(s32[4]{0:T(128)} %bitcast.93, bf16[192,2560]{1,0:T(8,128)(2,1)} %fusion.23.qT, bf16[2560,384]{1,0:T(8,128)(2,1)} %get-tuple-element.59.kn, bf16[2560,384]{1,0:T(8,128)(2,1)} %get-tuple-element.58.vn, ...), custom_call_target="tpu_custom_call" | custom-call | tf_op jit(solution)/shard_map/attention_backward/pallas_call | solution.py:228
  820.5 8.2 fusion.97
  828.9 8.0 fusion.81
  836.8 8.9 fusion.27
  845.9 2.7 fusion.83
  848.5 1.3 constant_dynamic-update-slice_fusion.2
  849.9 1.8 fusion.37
  851.7 1.1 fusion.33
  852.8 1.6 constant_dynamic-update-slice_fusion.1
  854.3 1.6 constant_dynamic-update-slice_fusion
  855.9 4.6 broadcast_in_dim.38
  860.5 15.4 %scatter_fusion = f32[16,192,768]{2,1,0:T(8,128)} fusion(f32[16,192,768]{2,1,0:T(8,128)} %broadcast_in_dim.38, s32[13]{0:T(128)S(1)} %copy-done.25, f32[13,192,768]{2,1,0:T(8,128)} %constant_dynamic-update-slice_fusion), kind=kCustom, calls=%fused_computation.1 | custom fusion | bytes 23003188 | tf_op jit(solution)/shard_map/scatter | solution.py:457
  880.5 101.4 %all-reduce.16.cloned.1.call-done = f32[2560,768]{1,0:T(8,128)} async-done(((f32[2560,768]{1,0:T(8,128)}), f32[2560,768]{1,0:T(8,128)}) %all-reduce.16.cloned.1.call-update) | async-done | bytes 7864336 | tf_op jit(solution)/shard_map/psum | solution.py:429
  981.9 5.9 fusion.17
  987.9 40.2 %all-reduce.3 = (f32[]{:T(128)}, f32[32,3]{0,1:T(4,128)S(1)}, f32[3,768]{1,0:T(4,128)S(1)}, f32[1]{0:T(128)}) all-reduce(f32[]{:T(128)S(6)} %div.85, f32[32,3]{0,1:T(4,128)S(1)} %fusion.41, f32[3,768]{1,0:T(4,128)S(1)} %pad_maximum_fusion, f32[1]{0:T(128)} %bitcast.21), channel_id=1, replica_groups=mesh['wide'=8,'narrow'=4] {'wide'}, use_global_device_ids=true, to_apply=%region_12.13 | all-reduce | flops 2402 | bytes 19216 | tf_op jit(solution)/shard_map/psum | solution.py:445
  1032.5 116.8 %reduce-scatter.2.cloned.1.call-done = f32[2,192,768]{2,1,0:T(8,128)} async-done(((f32[16,192,768]{2,1,0:T(8,128)}), f32[2,192,768]{2,1,0:T(8,128)}) %reduce-scatter.2.cloned.1.call-update) | async-done | bytes 1179664 | tf_op jit(solution)/shard_map/reduce_scatter | solution.py:459
  1149.3 2.2 multiply_reduce_fusion.6
  1152.1 11.3 fusion.6
  1163.4 39.3 %psum.79 = f32[]{:T(128)} all-reduce(f32[]{:T(128)S(6)} %add.224), channel_id=1, replica_groups=mesh['wide'=8,'narrow'=4] {'wide','narrow'}, use_global_device_ids=true, to_apply=%region_33.34 | all-reduce | flops 1 | bytes 8 | tf_op jit(solution)/shard_map/psum | solution.py:471
  1204.2 1.3 multiply_subtract_fusion.3
  1205.6 1.4 multiply_subtract_fusion.2
  1207.0 3.7 multiply_subtract_fusion.1
  (132 shorter events, 10.2 us)
Async XLA Ops:
  7.2 11.5 copy-start.26
  7.2 11.7 copy-start.30
  7.2 11.8 copy-start.20
  7.2 86.2 %all-gather.4.cloned.1.call-start = ((), (), s32[]{:S(2)}) async-start(), calls=%async_computation.1 | async-start | bytes 5308416 | tf_op jit(solution)/shard_map/all_gather | solution.py:275
  9.4 284.6 %all-reduce.10.cloned.1.call-start = ((), (), s32[]{:S(2)}) async-start(), calls=%async_computation.2 | async-start | bytes 15728640 | tf_op jit(solution)/shard_map/psum | solution.py:324
  10.4 88.1 %copy-start.21 = (s32[2304]{0:T(1024)}, s32[2304]{0:T(1024)S(1)}, u32[]{:S(2)}) copy-start(s32[2304]{0:T(1024)S(1)} %pad.9) | copy-start | bytes 27652
  18.9 82.8 %copy-start.24 = (s32[13]{0:T(128)}, s32[13]{0:T(128)S(1)}, u32[]{:S(2)}) copy-start(s32[13]{0:T(128)S(1)} %compare_select_fusion) | copy-start | bytes 160
  98.5 3.4 copy-start.3
  101.8 36.7 %copy-start.7 = (bf16[13,192,768]{2,1,0:T(8,128)(2,1)}, bf16[13,192,768]{2,1,0:T(8,128)(2,1)S(1)}, u32[]{:S(2)}) copy-start(bf16[13,192,768]{2,1,0:T(8,128)(2,1)S(1)} %select_convert_fusion) | copy-start | bytes 11501572
  101.9 7.1 copy-start.17
  144.2 314.3 %all-reduce.12.cloned.1.call-start = ((), (), s32[]{:S(2)}) async-start(), calls=%async_computation.3 | async-start | bytes 15728640 | tf_op jit(solution)/shard_map/psum | solution.py:331
  146.3 153.2 %copy-start.13 = (bf16[4,192,768]{2,1,0:T(8,128)(2,1)}, bf16[4,192,768]{2,1,0:T(8,128)(2,1)S(1)}, u32[]{:S(2)}) copy-start(bf16[4,192,768]{2,1,0:T(8,128)(2,1)S(1)} %get-tuple-element.60) | copy-start | bytes 3538948
  146.3 156.7 %copy-start.15 = (bf16[4,192,768]{2,1,0:T(8,128)(2,1)}, bf16[4,192,768]{2,1,0:T(8,128)(2,1)S(1)}, u32[]{:S(2)}) copy-start(bf16[4,192,768]{2,1,0:T(8,128)(2,1)S(1)} %get-tuple-element.61) | copy-start | bytes 3538948
  299.5 3.5 copy-start
  302.9 3.1 copy-start.32
  312.9 0.8 copy-start.27
  312.9 267.0 %all-reduce.18.cloned.1.call-start = ((), (), s32[]{:S(2)}) async-start(), calls=%async_computation.7 | async-start | bytes 196608
  464.9 3.2 copy-start.1
  464.9 45.3 %copy-start.31 = (u32[32]{0:T(128)S(1)}, u32[32]{0:T(128)}, u32[]{:S(2)}) copy-start(u32[32]{0:T(128)} %constant.152) | copy-start | bytes 388
  510.2 254.4 %all-reduce.14.cloned.1.call-start = ((), (), s32[]{:S(2)}) async-start(), calls=%async_computation.4 | async-start | bytes 15728640 | tf_op jit(solution)/shard_map/psum | solution.py:401
  592.7 12.5 %slice-start.2 = ((s8[7864320]{0:T(1024)(128)(4,1)}), s8[4194304]{0:T(1024)(128)(4,1)S(1)}, s32[]{:S(2)}) async-start(s8[7864320]{0:T(1024)(128)(4,1)} %bitcast.97), calls=%async_computation.10 | async-start | bytes 8388608
  600.7 4.6 copy-start.16
  600.7 4.7 slice-start.3
  605.4 7.5 copy-start.6
  605.4 9.4 copy-start.14
  612.9 1.9 copy-start.11
  620.1 361.8 %all-reduce.16.cloned.1.call-start = ((), (), s32[]{:S(2)}) async-start(), calls=%async_computation.5 | async-start | bytes 15728640 | tf_op jit(solution)/shard_map/psum | solution.py:429
  764.7 7.8 copy-start.5
  779.3 3.1 copy-start.2
  785.7 34.8 %copy-start.18 = (bf16[3,192,768]{2,1,0:T(8,128)(2,1)S(1)}, bf16[3,192,768]{2,1,0:T(8,128)(2,1)}, u32[]{:S(2)}) copy-start(bf16[3,192,768]{2,1,0:T(8,128)(2,1)} %copy-done.17) | copy-start | bytes 2654212
  828.8 320.4 %reduce-scatter.2.cloned.1.call-start = ((), (), s32[]{:S(2)}) async-start(), calls=%async_computation.6 | async-start | bytes 10616832 | tf_op jit(solution)/shard_map/reduce_scatter | solution.py:459
  836.8 8.9 copy-start.4
  836.8 9.0 copy-start.28
  845.7 4.1 slice-start
  845.9 4.0 slice-start.1
  845.9 4.0 copy-start.8
  854.3 6.2 copy-start.25
  875.9 4.0 copy-start.22
  875.9 4.0 copy-start.29
  1028.1 124.0 %copy-start.19 = (f32[3,768]{1,0:T(4,128)}, f32[3,768]{1,0:T(4,128)S(1)}, u32[]{:S(2)}) copy-start(f32[3,768]{1,0:T(4,128)S(1)} %get-tuple-element.41) | copy-start | bytes 27652
  1028.1 124.0 %copy-start.23 = (f32[32,3]{0,1:T(4,128)}, f32[32,3]{0,1:T(4,128)S(1)}, u32[]{:S(2)}) copy-start(f32[32,3]{0,1:T(4,128)S(1)} %get-tuple-element.40) | copy-start | bytes 1156
  1152.1 54.8 %copy-start.9 = (f32[2,192,768]{2,1,0:T(8,128)S(1)}, f32[2,192,768]{2,1,0:T(8,128)}, u32[]{:S(2)}) copy-start(f32[2,192,768]{2,1,0:T(8,128)} %param.20) | copy-start | bytes 3538948
  1152.1 54.8 %copy-start.10 = (f32[2,192,768]{2,1,0:T(8,128)S(1)}, f32[2,192,768]{2,1,0:T(8,128)}, u32[]{:S(2)}) copy-start(f32[2,192,768]{2,1,0:T(8,128)} %reduce-scatter.2.cloned.1.call-done) | copy-start | bytes 3538948
  1152.1 54.8 %copy-start.12 = (f32[2,192,768]{2,1,0:T(8,128)S(1)}, f32[2,192,768]{2,1,0:T(8,128)}, u32[]{:S(2)}) copy-start(f32[2,192,768]{2,1,0:T(8,128)} %param.22) | copy-start | bytes 3538948
Sparse Core Ops, SparseCore 0:
  10.8 82.5 all-gather.3
  144.3 149.6 all-reduce.9
  313.1 145.4 all-reduce.11
  510.3 69.5 all-reduce.17
  620.2 144.3 all-reduce.13
  828.9 152.9 all-reduce.15
  985.5 163.7 reduce-scatter.1

commit v2 on v0

v2 whole, which is shorter than its diff:
```python
import jax
import jax.numpy as jnp
from jax import lax
from jax.experimental import pallas as pl
from jax.experimental.pallas import tpu as pltpu
from jax.sharding import PartitionSpec as P

D = 768
FF = 3072
BUCKETS = 32
TOK_DEV = 2560
SEQS_DEV = 4
DOCLEN = 1024
CAP = 2
STEP = 10
LANE = 128
BQ = 512
BK = 512
REACH = DOCLEN // LANE
OFF = REACH + (BQ + BK) // LANE
SPAN = 2 * OFF + 1
LINES = 2 * REACH + 2
VMEM_LIMIT = 56 * 1024 * 1024

norm_eps = 1e-06
clip_limit = 0.01
learn_rate = 0.01
side_rate = 0.5
beta_one = 0.5
beta_two = 0.5
adam_eps = 1e-08
decay_rate = 0.01
score_scale = 0.125
masked_score = -1e30
low_type = jnp.bfloat16


def times_transposed(left_side, right_side):
    return lax.dot_general(
        left_side, right_side, (((1,), (1,)), ((), ())), preferred_element_type=jnp.float32
    )


def plain_product(left_side, right_side):
    return jnp.dot(left_side, right_side, preferred_element_type=jnp.float32)


def outer_product(left_side, right_side):
    return lax.dot_general(
        left_side, right_side, (((0,), (0,)), ((), ())), preferred_element_type=jnp.float32
    )


def rms_scale(values):
    return lax.rsqrt(jnp.mean(values * values, axis=-1, keepdims=True) + norm_eps)


def norm_backward(values, row_scale, gain_row, grad_out):
    weighted = grad_out * gain_row
    gain_grad = jnp.sum(grad_out * values * row_scale, axis=0)
    inner_mean = jnp.mean(weighted * values, axis=-1, keepdims=True)
    value_grad = row_scale * weighted - values * row_scale * row_scale * row_scale * inner_mean
    return (value_grad, gain_grad)


def decoupled_decay_step(gradient, first_moment, second_moment, weight, multiplier, step_rate):
    clipped = gradient * multiplier
    first_new = beta_one * first_moment + (1.0 - beta_one) * clipped
    second_new = beta_two * second_moment + (1.0 - beta_two) * clipped * clipped
    first_hat = first_new / (1.0 - beta_one**STEP)
    second_hat = second_new / (1.0 - beta_two**STEP)
    weight_new = weight - step_rate * (
        first_hat / (jnp.sqrt(second_hat) + adam_eps) + decay_rate * weight
    )
    return (first_new, second_new, weight_new)


def swap(values, bit):
    count = lax.axis_size("narrow")
    return lax.ppermute(values, "narrow", [(i, i ^ bit) for i in range(count)])


def narrow_bits():
    count = lax.axis_size("narrow")
    return [1 << s for s in range(count.bit_length() - 1)]


def peer_order():
    order = [0]
    for bit in reversed(narrow_bits()):
        order = order + [peer ^ bit for peer in order]
    return order


def join_rows(values):
    for bit in reversed(narrow_bits()):
        values = jnp.concatenate([values, swap(values, bit)], axis=0)
    return values


def add_rows(values):
    for bit in narrow_bits():
        half = values.shape[0] // 2
        came = swap(values[half:].astype(low_type), bit)
        values = values[:half].astype(jnp.float32) + came.astype(jnp.float32)
    return values


def product_add_rows(left_side, right_side):
    bits = narrow_bits()
    half = left_side.shape[0] // 2
    sent = plain_product(left_side[half:], right_side).astype(low_type)
    came = swap(sent, bits[0])
    values = plain_product(left_side[:half], right_side) + came.astype(jnp.float32)
    for bit in bits[1:]:
        half = values.shape[0] // 2
        came = swap(values[half:].astype(low_type), bit)
        values = values[:half] + came.astype(jnp.float32)
    return values


def natural_rows(joined, narrow_index):
    order = peer_order()
    group = joined.shape[0] // len(order)
    place = jnp.array([order.index(peer) for peer in range(len(order))], jnp.int32)
    return jnp.concatenate(
        [
            lax.dynamic_slice_in_dim(joined, place[g ^ narrow_index] * group, group, 0)
            for g in range(len(order))
        ],
        axis=0,
    )


def spread(values):
    count = lax.axis_size("wide") * lax.axis_size("narrow")
    copies = jnp.broadcast_to(values[None], (count,) + values.shape)
    return lax.all_to_all(copies, ("wide", "narrow"), split_axis=0, concat_axis=0, tiled=True)


def smem():
    return pl.BlockSpec(memory_space=pltpu.SMEM)


def vmem():
    return pl.BlockSpec(memory_space=pltpu.VMEM)


def bias_kernel(chunks, tiles):
    heads = tiles.shape[0]
    tiles[...] = jnp.zeros_like(tiles)
    for h in range(heads):
        for d in range(-REACH, REACH + 1):
            left = chunks[h, REACH + 1 - d : REACH + 2 - d, :]
            right = chunks[h, REACH - d : REACH + 1 - d, :]
            line = jnp.broadcast_to(jnp.concatenate([left, right], axis=1), (LANE, 2 * LANE))
            rolled = pltpu.roll(line, 0, 1, stride=1, stride_axis=0)
            tiles[h, (d + OFF) * LANE : (d + OFF + 1) * LANE, :] = rolled[:, :LANE]


def bias_tiles(rel_chunks):
    heads = rel_chunks.shape[0]
    return pl.pallas_call(
        bias_kernel,
        out_shape=jax.ShapeDtypeStruct((heads, SPAN * LANE, LANE), jnp.float32),
        compiler_params=pltpu.CompilerParams(vmem_limit_bytes=VMEM_LIMIT),
        name="bias_tiles",
    )(rel_chunks)


def key_range(lengths, first, last):
    start = jnp.int32(0)
    low = jnp.int32(0)
    high = jnp.int32(0)
    for s in range(SEQS_DEV):
        end = start + lengths[s]
        low = jnp.where(start <= first, start, low)
        high = jnp.where(start <= last, end, high)
        start = end
    return low // BK, (high + BK - 1) // BK


def bias_part(bias, h, row):
    return jnp.concatenate(
        [
            bias[h, pl.ds(pl.multiple_of(row - b * LANE, LANE), BK), :]
            for b in range(BQ // LANE)
        ],
        axis=1,
    )


def forward_kernel(first_row, lengths, origin, qT, kn, vT, apart, bias, ctx_o, ctxT_o, lse_o, qa, acc):
    width, rows_here = qT.shape
    heads = bias.shape[0]
    size = width // heads
    qa[...] = jnp.zeros_like(qa)

    @pl.loop(0, rows_here // BQ)
    def _(i):
        q0 = pl.multiple_of(i * BQ, BQ)
        here = pl.ds(q0, BQ)
        for h in range(heads):
            qa[h * LANE : h * LANE + size, :] = qT[h * size : (h + 1) * size, here]
            qa[h * LANE + size : h * LANE + size + 16, :] = apart[:, here]
        acc[...] = jnp.zeros_like(acc)
        low, high = key_range(lengths, first_row + q0, first_row + q0 + BQ - 1)

        def step(j, carry):
            k0 = pl.multiple_of(j * BK, BK)
            row = (j * (BK // LANE) - i * (BQ // LANE) - first_row // LANE + OFF) * LANE
            out = []
            for h in range(heads):
                top, total = carry[2 * h], carry[2 * h + 1]
                own = slice(h * LANE, (h + 1) * LANE)
                rows = slice(h * size, (h + 1) * size)
                s = plain_product(kn[pl.ds(k0, BK), own], qa[own, :]) + bias_part(bias, h, row)
                new_top = jnp.maximum(top, jnp.max(s, axis=0, keepdims=True))
                fade = jnp.exp(top - new_top)
                p = jnp.exp(s - new_top)
                total = total * fade + jnp.sum(p, axis=0, keepdims=True)
                acc[rows, :] = acc[rows, :] * fade + plain_product(
                    vT[rows, pl.ds(k0, BK)], p.astype(low_type)
                )
                out += [new_top, total]
            return tuple(out)

        init = tuple(
            jnp.full((1, BQ), 2.0 * masked_score if n % 2 == 0 else 0.0, jnp.float32)
            for n in range(2 * heads)
        )
        done = lax.fori_loop(low, high, step, init)
        for h in range(heads):
            rows = slice(h * size, (h + 1) * size)
            acc[rows, :] = acc[rows, :] / done[2 * h + 1]
            lse_o[h : h + 1, here] = done[2 * h] + jnp.log(done[2 * h + 1])
        ctxT_o[:, here] = acc[...]
        turned = acc[...].T.astype(low_type)
        for b in range(BQ // LANE):
            at = pl.multiple_of(origin[i * (BQ // LANE) + b], LANE)
            ctx_o[pl.ds(at, LANE), :] = turned[b * LANE : (b + 1) * LANE, :]


def attention_forward(first_row, lengths, origin, qT, kn, vT, apart, bias):
    width, rows_here = qT.shape
    heads = bias.shape[0]

    def body(*refs):
        forward_kernel(first_row, *refs)

    return pl.pallas_call(
        body,
        out_shape=(
            jax.ShapeDtypeStruct((rows_here, width), low_type),
            jax.ShapeDtypeStruct((width, rows_here), jnp.float32),
            jax.ShapeDtypeStruct((heads, rows_here), jnp.float32),
        ),
        in_specs=[smem()] * 2 + [vmem()] * 5,
        out_specs=(vmem(),) * 3,
        scratch_shapes=[
            pltpu.VMEM((heads * LANE, BQ), low_type),
            pltpu.VMEM((width, BQ), jnp.float32),
        ],
        compiler_params=pltpu.CompilerParams(vmem_limit_bytes=VMEM_LIMIT),
        cost_estimate=pl.CostEstimate(
            flops=8 * rows_here * TOK_DEV * width,
            bytes_accessed=12 * width * TOK_DEV,
            transcendentals=rows_here * TOK_DEV * heads,
        ),
        name="attention_forward",
    )(lengths, origin, qT, kn, vT, apart, bias)


def three_parts(values):
    first = values.astype(low_type).astype(jnp.float32)
    rest = values - first
    second = rest.astype(low_type).astype(jnp.float32)
    return first, second, rest - second


def backward_kernel(
    lengths, origin, qT, kn, vn, kT, dcn, ctxT, lse, apart, bias,
    dT_o, dn_o, lines_o, qa, da, dq, dk, dv, tiles,
):
    width, tokens = qT.shape
    heads = bias.shape[0]
    size = width // heads
    for ref in (qa, da, dk, dv, tiles):
        ref[...] = jnp.zeros_like(ref)
    place = lax.broadcasted_iota(jnp.int32, (16, BQ), 0) - SEQS_DEV

    def in_depth(values):
        a, b, c = three_parts(values)
        return jnp.where(place == 0, a, jnp.where(place == 1, b, jnp.where(place == 2, c, 0.0)))

    @pl.loop(0, tokens // BQ)
    def _(i):
        q0 = pl.multiple_of(i * BQ, BQ)
        here = pl.ds(q0, BQ)
        at = [pl.multiple_of(origin[i * (BQ // LANE) + b], LANE) for b in range(BQ // LANE)]
        dcT = jnp.concatenate(
            [dcn[pl.ds(at[b], LANE), :].astype(jnp.float32) for b in range(BQ // LANE)], axis=0
        ).T
        for h in range(heads):
            rows = slice(h * size, (h + 1) * size)
            top = h * LANE
            qa[top : top + size, :] = qT[rows, here]
            extra = apart[:, here].astype(jnp.float32) + in_depth(-lse[h : h + 1, here])
            qa[top + size : top + size + 16, :] = extra.astype(low_type)
            da[top : top + size, :] = dcT[rows, :].astype(low_type)
            delta = jnp.sum(dcT[rows, :] * ctxT[rows, here], axis=0, keepdims=True)
            da[top + size : top + size + 16, :] = in_depth(-delta).astype(low_type)
        dq[...] = jnp.zeros_like(dq)
        low, high = key_range(lengths, q0, q0 + BQ - 1)

        @pl.loop(low, high)
        def _(j):
            k0 = pl.multiple_of(j * BK, BK)
            there = pl.ds(k0, BK)
            row = (j * (BK // LANE) - i * (BQ // LANE) + OFF) * LANE
            for h in range(heads):
                rows = slice(h * size, (h + 1) * size)
                own = slice(h * LANE, (h + 1) * LANE)
                flat = slice(h * LANE, h * LANE + size)
                s = plain_product(kn[there, own], qa[own, :])
                p = jnp.exp(s + bias_part(bias, h, row))
                ds = p * plain_product(vn[there, own], da[own, :])
                for b in range(BQ // LANE):
                    window = pl.ds(pl.multiple_of(row - b * LANE, LANE), BK)
                    tiles[h, window, :] = (
                        tiles[h, window, :] + ds[:, b * LANE : (b + 1) * LANE]
                    )
                p_low = p.astype(low_type)
                ds_low = ds.astype(low_type)
                dv[rows, there] = dv[rows, there] + times_transposed(da[flat, :], p_low)
                dk[rows, there] = dk[rows, there] + times_transposed(qa[flat, :], ds_low)
                dq[rows, :] = dq[rows, :] + plain_product(kT[rows, there], ds_low)

        grad = dq[...] * score_scale
        dT_o[0:width, here] = grad.astype(low_type)
        turned = grad.T.astype(low_type)
        for b in range(BQ // LANE):
            dn_o[pl.ds(at[b], LANE), 0:width] = turned[b * LANE : (b + 1) * LANE, :]

    @pl.loop(0, tokens // BQ)
    def _(i):
        here = pl.ds(pl.multiple_of(i * BQ, BQ), BQ)
        both = jnp.concatenate([dk[:, here], dv[:, here]], axis=0)
        dT_o[width : 3 * width, here] = both.astype(low_type)
        turned = both.T.astype(low_type)
        for b in range(BQ // LANE):
            at = pl.multiple_of(origin[i * (BQ // LANE) + b], LANE)
            dn_o[pl.ds(at, LANE), width : 3 * width] = turned[b * LANE : (b + 1) * LANE, :]

    across = lax.broadcasted_iota(jnp.int32, (LANE, LANE), 1)
    over = across >= lax.broadcasted_iota(jnp.int32, (LANE, LANE), 0)
    sub = lax.broadcasted_iota(jnp.int32, (8, LANE), 0)
    for h in range(heads):
        for d in range(-REACH, REACH + 2):
            here = tiles[h, (d + OFF) * LANE : (d + OFF + 1) * LANE, :]
            below = tiles[h, (d + OFF - 1) * LANE : (d + OFF) * LANE, :]
            mixed = jnp.where(over, here, below)
            line = mixed[LANE - 8 :, :]
            for g in range(LANE // 8 - 2, -1, -1):
                line = mixed[8 * g : 8 * g + 8, :] + pltpu.roll(line, LANE - 8, 1)
            for bit in (1, 2, 4):
                line = jnp.where((sub & bit) != 0, pltpu.roll(line, LANE - bit, 1), line)
            lines_o[h, REACH + 1 - d : REACH + 2 - d, :] = jnp.sum(line, axis=0, keepdims=True)


def attention_backward(lengths, origin, qT, kn, vn, kT, dcn, ctxT, lse, apart, bias):
    width, tokens = qT.shape
    heads = bias.shape[0]
    return pl.pallas_call(
        backward_kernel,
        out_shape=(
            jax.ShapeDtypeStruct((3 * width, tokens), low_type),
            jax.ShapeDtypeStruct((tokens, 3 * width), low_type),
            jax.ShapeDtypeStruct((heads, LINES, LANE), jnp.float32),
        ),
        in_specs=[smem()] * 2 + [vmem()] * 9,
        out_specs=(vmem(),) * 3,
        scratch_shapes=[
            pltpu.VMEM((heads * LANE, BQ), low_type),
            pltpu.VMEM((heads * LANE, BQ), low_type),
            pltpu.VMEM((width, BQ), jnp.float32),
            pltpu.VMEM((width, tokens), jnp.float32),
            pltpu.VMEM((width, tokens), jnp.float32),
            pltpu.VMEM((heads, SPAN * LANE, LANE), jnp.float32),
        ],
        compiler_params=pltpu.CompilerParams(vmem_limit_bytes=VMEM_LIMIT),
        cost_estimate=pl.CostEstimate(
            flops=20 * tokens * TOK_DEV * width,
            bytes_accessed=30 * width * TOK_DEV,
            transcendentals=tokens * TOK_DEV * heads,
        ),
        name="attention_backward",
    )(lengths, origin, qT, kn, vn, kT, dcn, ctxT, lse, apart, bias)


def on_device(
    layer_argument,
    document_extents,
    distance_bin_lookup,
    tile_location,
    precise_parameter_blocks,
    precise_mean_est,
    precise_variance_est,
    rescaling_coefficients,
    norm_scale_mean_est,
    norm_scale_variance_est,
    distance_bias_table,
    offset_bias_mean_est,
    offset_bias_variance_est,
    sharpness_exponent,
    sharpness_mean_est,
    sharpness_variance_est,
):
    wide_count = lax.axis_size("wide")
    narrow_count = lax.axis_size("narrow")
    wide_index = lax.axis_index("wide")
    narrow_index = lax.axis_index("narrow")
    order = peer_order()
    place_of = jnp.array([order.index(peer) for peer in range(narrow_count)], jnp.int32)
    unit_rows = precise_parameter_blocks.shape[1]
    heads_here = distance_bias_table.shape[1]
    head_size = unit_rows // heads_here
    ffn_units = FF // D
    group = TOK_DEV // narrow_count
    own_slots = wide_index * CAP + jnp.arange(CAP, dtype=jnp.int32)

    every_slot = lax.all_gather(
        precise_parameter_blocks.astype(low_type), "wide", axis=0, tiled=True
    )

    def block(u):
        return lax.dynamic_index_in_dim(every_slot, tile_location[u], 0, keepdims=False)

    qkv_weight = jnp.concatenate([block(u) for u in range(3)], axis=0)
    inner_weight = jnp.concatenate([block(5 + k) for k in range(ffn_units)], axis=0)
    outer_weight = jnp.concatenate([block(5 + ffn_units + k) for k in range(ffn_units)], axis=0)
    both_joined = join_rows(jnp.stack([block(3), block(4)])[None])
    out_joined = both_joined[:, 0].reshape(D, D)
    proj_weight = natural_rows(both_joined[:, 1].reshape(D, D), narrow_index)

    lengths = document_extents[0]
    seq_ends = jnp.cumsum(lengths)
    positions = jnp.arange(TOK_DEV, dtype=jnp.int32)

    def segments_of(where):
        return jnp.sum((seq_ends[None, :] <= where[:, None]).astype(jnp.int32), axis=1)

    segment_ids = segments_of(positions)
    peers = jnp.array(order, jnp.int32)[positions // group]
    joined_segments = segments_of((peers ^ narrow_index) * group + positions % group)
    own_segments = joined_segments[:group]
    tile_starts = jnp.arange(TOK_DEV // LANE, dtype=jnp.int32) * LANE
    origin = place_of[(tile_starts // group) ^ narrow_index] * group + tile_starts % group

    beyond = LINES * LANE - LANE - 1 - distance_bin_lookup.shape[0]
    offsets_down = jnp.pad(distance_bin_lookup[::-1], (LANE + 1, beyond), constant_values=-1)
    bucket_onehot = (
        offsets_down[:, None] == jnp.arange(BUCKETS, dtype=jnp.int32)[None, :]
    ).astype(jnp.float32)
    rel_values = jnp.dot(bucket_onehot, distance_bias_table, precision=lax.Precision.HIGHEST).T
    tiles_bias = bias_tiles(rel_values.reshape(heads_here, LINES, LANE))

    all_rows = layer_argument.astype(jnp.float32)
    normed_one = (all_rows * rms_scale(all_rows) * rescaling_coefficients[0]).astype(low_type)
    transposed_rows = times_transposed(qkv_weight, normed_one)
    query_cols = (transposed_rows[:unit_rows] * score_scale).astype(low_type)
    key_cols = transposed_rows[unit_rows : 2 * unit_rows].astype(low_type)
    value_cols = transposed_rows[2 * unit_rows :].astype(low_type)
    spread_weight = jnp.pad(
        qkv_weight[unit_rows:].reshape(2 * heads_here, head_size, D),
        ((0, 0), (0, LANE - head_size), (0, 0)),
    ).reshape(2 * heads_here * LANE, D)
    lane_place = jnp.arange(2 * heads_here * LANE, dtype=jnp.int32) % LANE - head_size
    marks = jnp.logical_or(
        lane_place[None, :] == segment_ids[:, None],
        jnp.logical_and(lane_place >= SEQS_DEV, lane_place < SEQS_DEV + 3)[None, :],
    )
    key_value_rows = (
        times_transposed(normed_one, spread_weight) + marks.astype(jnp.float32)
    ).astype(low_type)
    key_rows = key_value_rows[:, : heads_here * LANE]
    value_rows = key_value_rows[:, heads_here * LANE :]
    row_place = jnp.arange(16, dtype=jnp.int32)[:, None]
    apart = jnp.where(
        jnp.logical_and(row_place < SEQS_DEV, row_place != segment_ids[None, :]), masked_score, 0.0
    ).astype(low_type)
    context, context_cols, log_rows = attention_forward(
        0, lengths, origin, query_cols, key_rows, value_cols, apart, tiles_bias
    )

    def to_peer(values, peer):
        if peer == 0:
            return values
        pairs = [(i, i ^ peer) for i in range(narrow_count)]
        return lax.ppermute(values, "narrow", pairs)

    context_own = jnp.concatenate(
        [
            to_peer(context[s * group : (s + 1) * group], peer)
            for s, peer in enumerate(order)
        ],
        axis=1,
    )
    own_rows = lax.dynamic_slice_in_dim(layer_argument, narrow_index * group, group, 0).astype(
        jnp.float32
    )
    scale_one = rms_scale(own_rows)
    residual_mid = own_rows + plain_product(context_own, out_joined)
    scale_two = rms_scale(residual_mid)
    normed_two_own = (residual_mid * scale_two * rescaling_coefficients[1]).astype(low_type)
    normed_two = join_rows(normed_two_own)

    gate_pre = times_transposed(normed_two, inner_weight)
    hidden_act, gelu_back = jax.vjp(jax.nn.gelu, gate_pre)
    hidden_low = hidden_act.astype(low_type)
    result_own = residual_mid + product_add_rows(hidden_low, outer_weight)
    result_joined = join_rows(result_own.astype(low_type))
    layer_result = natural_rows(result_joined, narrow_index).astype(jnp.float32)

    scale_three = rms_scale(result_own)
    member = (
        own_segments[None, :] == jnp.arange(SEQS_DEV, dtype=jnp.int32)[:, None]
    ).astype(jnp.float32)
    length_values = lengths.astype(jnp.float32)[:, None]
    unscaled_part = (
        jnp.dot(member, result_own * scale_three, precision=lax.Precision.HIGHEST) / length_values
    )
    total_seqs = wide_count * SEQS_DEV
    unscaled = jnp.sum(
        spread(unscaled_part).reshape(wide_count, narrow_count, SEQS_DEV, D), axis=1
    ).reshape(total_seqs, D)
    pooled_low = (unscaled * rescaling_coefficients[2]).astype(low_type)
    projected = times_transposed(pooled_low, proj_weight).astype(low_type).astype(jnp.float32)
    inverse = lax.rsqrt(jnp.sum(projected * projected, axis=1, keepdims=True) + norm_eps)
    embed_low = (projected * inverse).astype(low_type)
    embeddings = embed_low.astype(jnp.float32)
    sharpness_factor = jnp.exp(sharpness_exponent[0])
    angular_agreement = times_transposed(embed_low, embed_low)
    seq_index = jnp.arange(total_seqs, dtype=jnp.int32)
    sharpened_agreement = jnp.where(
        seq_index[None, :] == seq_index[:, None],
        masked_score,
        sharpness_factor * angular_agreement,
    )
    row_top = jnp.max(sharpened_agreement, axis=1, keepdims=True)
    log_total = row_top + jnp.log(
        jnp.sum(jnp.exp(sharpened_agreement - row_top), axis=1, keepdims=True)
    )
    partner = seq_index[None, :] == jnp.bitwise_xor(seq_index, 1)[:, None]
    positive = jnp.sum(jnp.where(partner, sharpened_agreement, 0.0), axis=1)
    loss = jnp.mean(log_total[:, 0] - positive)
    raw_score_slope = (
        jnp.exp(sharpened_agreement - log_total) - partner.astype(jnp.float32)
    ) / total_seqs
    sharpness_slope = sharpness_factor * jnp.sum(raw_score_slope * angular_agreement)
    embed_grad = sharpness_factor * jnp.dot(
        raw_score_slope + raw_score_slope.T, embeddings, precision=lax.Precision.HIGHEST
    )
    along = jnp.sum(projected * embed_grad, axis=1, keepdims=True)
    proj_grad_low = (
        inverse * embed_grad - projected * inverse * inverse * inverse * along
    ).astype(low_type)
    proj_weight_grad = outer_product(
        lax.dynamic_slice_in_dim(proj_grad_low, narrow_index * unit_rows, unit_rows, 1), pooled_low
    )
    pooled_grad = plain_product(proj_grad_low, proj_weight)
    final_gain_grad = jnp.sum(pooled_grad * unscaled, axis=0)
    own_pooled_grad = lax.dynamic_slice_in_dim(
        pooled_grad, wide_index * SEQS_DEV, SEQS_DEV, 0
    ) * (rescaling_coefficients[2] / length_values)

    def final_backward(values, segments):
        weighted = own_pooled_grad[SEQS_DEV - 1]
        for s in range(SEQS_DEV - 2, -1, -1):
            weighted = jnp.where((segments == s)[:, None], own_pooled_grad[s], weighted)
        row_scale = rms_scale(values)
        inner_mean = jnp.mean(weighted * values, axis=-1, keepdims=True)
        return row_scale * weighted - values * (row_scale * row_scale * row_scale * inner_mean)

    encoded_grad = final_backward(result_own, own_segments)
    ffn_grad_low = final_backward(result_joined.astype(jnp.float32), joined_segments).astype(
        low_type
    )
    hidden_grad = times_transposed(ffn_grad_low, outer_weight)
    outer_grad = outer_product(hidden_low, ffn_grad_low)
    (pre_grad,) = gelu_back(hidden_grad)
    pre_low = pre_grad.astype(low_type)
    inner_grad = outer_product(pre_low, normed_two)
    normed_two_grad = product_add_rows(pre_low, inner_weight)
    mid_norm_grad, ffn_gain_grad = norm_backward(
        residual_mid, scale_two, rescaling_coefficients[1], normed_two_grad
    )
    mid_grad = encoded_grad + mid_norm_grad
    attn_grad_low = mid_grad.astype(low_type)
    out_grad = add_rows(outer_product(context_own, attn_grad_low))

    context_grad = jnp.concatenate(
        [
            to_peer(
                times_transposed(
                    attn_grad_low, out_joined[s * unit_rows : (s + 1) * unit_rows]
                ).astype(low_type),
                peer,
            )
            for s, peer in enumerate(order)
        ],
        axis=0,
    )
    qkv_cols, qkv_rows, bias_lines = attention_backward(
        lengths,
        origin,
        query_cols,
        key_rows,
        value_rows,
        key_cols,
        context_grad,
        context_cols,
        log_rows,
        apart,
        tiles_bias,
    )
    offset_bias_slope = lax.dot_general(
        bucket_onehot,
        bias_lines.reshape(heads_here, LINES * LANE),
        (((0,), (1,)), ((), ())),
        precision=lax.Precision.HIGHEST,
    )

    early = {3: out_grad}
    for k in range(ffn_units):
        rows = slice(k * unit_rows, (k + 1) * unit_rows)
        early[5 + k] = inner_grad[rows]
        early[5 + ffn_units + k] = outer_grad[rows]
    early_units = sorted(early)
    stacked = jnp.stack([early[u].astype(low_type) for u in early_units])
    slots = jnp.arange(wide_count * CAP, dtype=jnp.int32)
    held = slots[:, None] == tile_location[jnp.array(early_units)][None, :]
    source = jnp.sum(held * jnp.arange(len(early_units), dtype=jnp.int32)[None, :], axis=1)
    placed = jnp.where(
        jnp.any(held, axis=1)[:, None, None], stacked[source], jnp.zeros((), low_type)
    )
    slot_grads = lax.psum_scatter(placed, "wide", scatter_dimension=0, tiled=True).astype(
        jnp.float32
    )
    proj_here = (own_slots == tile_location[4]).astype(jnp.float32)
    slot_grads = slot_grads + proj_here[:, None, None] * proj_weight_grad[None]

    qkv_weight_grad = plain_product(qkv_cols, normed_one).astype(low_type)
    parts = lax.all_to_all(
        qkv_weight_grad.reshape(wide_count, 3 * unit_rows // wide_count, D),
        "wide",
        split_axis=0,
        concat_axis=0,
        tiled=True,
    )
    qkv_part = jnp.sum(parts.astype(jnp.float32), axis=0)
    qkv_whole = lax.all_gather(qkv_part.astype(low_type), "wide", axis=0, tiled=True).reshape(
        3, unit_rows, D
    )
    normed_one_grad = product_add_rows(qkv_rows, qkv_weight)
    input_norm_grad, attn_gain_grad = norm_backward(
        own_rows, scale_one, rescaling_coefficients[0], normed_one_grad
    )
    input_own = mid_grad + input_norm_grad
    input_grad = natural_rows(join_rows(input_own.astype(low_type)), narrow_index).astype(
        jnp.float32
    )

    bias_size = offset_bias_slope.size
    small = jnp.stack(
        [
            ffn_gain_grad,
            attn_gain_grad,
            jnp.pad(offset_bias_slope.reshape(bias_size), (0, D - bias_size)),
        ]
    )
    small_all = spread(small).reshape(wide_count, narrow_count, 3, D)
    gain_sums = jnp.sum(small_all[:, :, :2], axis=(0, 1))
    gain_total = jnp.stack([gain_sums[1], gain_sums[0], final_gain_grad])
    bias_all = jnp.sum(small_all[:, :, 2], axis=0)
    bias_total = lax.dynamic_index_in_dim(bias_all, narrow_index, 0, keepdims=False)[
        :bias_size
    ].reshape(offset_bias_slope.shape)
    sharpness_total = sharpness_slope.reshape(1)
    local_squares = jnp.sum(slot_grads * slot_grads) + jnp.sum(qkv_part * qkv_part)
    square_terms = spread(jnp.broadcast_to(local_squares, (8, LANE)))[:, 0, 0]
    grad_norm = jnp.sqrt(
        jnp.sum(square_terms)
        + jnp.sum(gain_total * gain_total)
        + jnp.sum(bias_all * bias_all)
        + sharpness_slope * sharpness_slope
    )
    multiplier = jnp.minimum(1.0, clip_limit / grad_norm)
    for u in range(3):
        here = (own_slots == tile_location[u])[:, None, None]
        slot_grads = jnp.where(here, qkv_whole[u].astype(jnp.float32)[None], slot_grads)
    slot_first, slot_second, slot_weight = decoupled_decay_step(
        slot_grads,
        precise_mean_est,
        precise_variance_est,
        precise_parameter_blocks,
        multiplier,
        learn_rate,
    )
    gain_first, gain_second, gain_new = decoupled_decay_step(
        gain_total,
        norm_scale_mean_est,
        norm_scale_variance_est,
        rescaling_coefficients,
        multiplier,
        side_rate,
    )
    bias_first, bias_second, bias_new = decoupled_decay_step(
        bias_total,
        offset_bias_mean_est,
        offset_bias_variance_est,
        distance_bias_table,
        multiplier,
        side_rate,
    )
    sharpness_mean_fresh, sharpness_variance_fresh, sharpness_exponent_fresh = decoupled_decay_step(
        sharpness_total,
        sharpness_mean_est,
        sharpness_variance_est,
        sharpness_exponent,
        multiplier,
        learn_rate,
    )
    return (
        loss,
        layer_result,
        input_grad,
        grad_norm,
        slot_first,
        slot_second,
        slot_weight,
        gain_first,
        gain_second,
        gain_new,
        bias_first,
        bias_second,
        bias_new,
        sharpness_mean_fresh,
        sharpness_variance_fresh,
        sharpness_exponent_fresh,
    )


def solution(mesh):
    placed = (
        P("wide", None),
        P("wide", None),
        P(),
        P(),
        P("wide", "narrow", None),
        P("wide", "narrow", None),
        P("wide", "narrow", None),
        P(),
        P(),
        P(),
        P(None, "narrow"),
        P(None, "narrow"),
        P(None, "narrow"),
        P(),
        P(),
        P(),
    )
    return jax.shard_map(
        on_device,
        mesh=mesh,
        in_specs=placed,
        out_specs=(
            P(),
            P("wide", None),
            P("wide", None),
            P(),
            P("wide", "narrow", None),
            P("wide", "narrow", None),
            P("wide", "narrow", None),
            P(),
            P(),
            P(),
            P(None, "narrow"),
            P(None, "narrow"),
            P(None, "narrow"),
            P(),
            P(),
            P(),
        ),
        check_vma=False,
    )
```

time: 2550 us -> 603 us (0.24); the launches traced: 2500 us -> 596 us
  local copies, waits for them, and re-layouts: 1230 us -> 38.6 us
  waiting for transfers between devices: 489 us -> 192 us
  matrix products: 346 us -> 68.2 us
  other arithmetic: 268 us -> 83.5 us
  Pallas kernels: 0 us -> 87.4 us
  blocking collectives: 121 us -> 38.1 us
  between operations: 28.6 us -> 58.6 us
  starting transfers between devices: 0.47 us -> 28.7 us
    unnamed x129 -> x213, local copies, waits for them, and re-layouts: 847 us -> 5.75 us
    psum x4 -> x0, waiting for transfers between devices: 421 us -> none  [the longest x1 146 us: on_device(): attn_total = lax.psum(plain_product(context, out_weight), 'narrow')]
    dot_general x40 -> x3, matrix products: 276 us -> 4.23 us  [the longest x1 1.89 us: on_device(): lax.dot_general(bucket_onehot, bias_lines.reshape(heads_here, LINES * LAN...]
    rev x2 -> x0, local copies, waits for them, and re-layouts: 240 us -> none  [the longest x1 120 us: diagonal_sums(): flipped = blocks[:, ::-1, :]]
    ppermute x0 -> x22, waiting for transfers between devices: none -> 145 us  [the longest x16 125 us: swap(): return lax.ppermute(values, 'narrow', [(i, i ^ bit) for i in range(count)])]
    add x9 -> x3, other arithmetic: 140 us -> 1.76 us  [the longest x1 1.16 us: add_rows(): values = values[:half].astype(jnp.float32) + came.astype(jnp.float32)]
    pallas_call x0 -> x3, Pallas kernels: none -> 87.4 us  [the longest x1 48 us: attention_backward(): pl.pallas_call(backward_kernel, out_shape=(jax.ShapeDtypeStruct((3 * widt...]
    psum x3 -> x0, blocking collectives: 85.5 us -> none  [the longest x1 38.2 us: on_device(): lax.psum((norm_scale_slopes, offset_bias_slope, sharpness_derivative.resh...]
  transfers between devices with their start and end apart: 7 -> 28, of which waited for: 4 -> 17; matrix products, arithmetic and copies ran while one was open for 48% -> 17% of each run, Pallas kernels for 0% -> 15%
where the time goes in v2:
time: 603 us; the launch traced here: 596 us
  waiting for transfers between devices  192 us (32%)
  Pallas kernels  87.4 us (14%)
  other arithmetic  83.5 us (14%)
  matrix products  68.2 us (11%)
  between operations  58.6 us (10%)
  local copies, waits for them, and re-layouts  38.6 us (6%)
  blocking collectives  38.1 us (6%)
  starting transfers between devices  28.7 us (5%)
    ppermute x16, waiting for transfers between devices, swap(): return lax.ppermute(values, 'narrow', [(i, i ^ bit) for i in range(count)])  125 us
    pallas_call x1, Pallas kernels, attention_backward(): pl.pallas_call(backward_kernel, out_shape=(jax.ShapeDtypeStruct((3 * widt...  48 us
    all_gather x1, waiting for transfers between devices, on_device(): lax.all_gather(precise_parameter_blocks.astype(low_type), 'wide', axis=0,...  44.5 us
    all_gather x1, blocking collectives, on_device(): lax.all_gather(qkv_part.astype(low_type), 'wide', axis=0, tiled=True)  38.1 us
    pallas_call x1, Pallas kernels, attention_forward(): pl.pallas_call(body, out_shape=(jax.ShapeDtypeStruct((rows_here, width),...  33.9 us
    dot_general x10, matrix products, times_transposed(): lax.dot_general(left_side, right_side, (((1,), (1,)), ((), ())), preferre...  32.1 us
    ppermute x6, waiting for transfers between devices, to_peer(): return lax.ppermute(values, 'narrow', pairs)  19.5 us
    dot_general x9, matrix products, plain_product(): return jnp.dot(left_side, right_side, preferred_element_type=jnp.float32)  18.9 us
  transfers between devices with their start and end apart: 28, of which 17 were waited for; matrix products, arithmetic and copies ran while one was open for 17% of the time, Pallas kernels for 15%

profile of v2, /device:TPU:0, one launch (start us, length us, event | category | flops | bytes accessed | tf_op | source)
XLA Modules:
  0.0 595.6 jit_solution(5150789309828089306)
XLA Ops:
  7.3 2.1 convert_element_type.195
  30.0 5.4 bias_tiles.1.refs_6_.bias
  45.2 3.0 fusion
  48.9 44.5 %all-gather.2.cloned.1.call-done = bf16[16,192,768]{2,1,0:T(8,128)(2,1)} async-done(((bf16[2,192,768]{2,1,0:T(8,128)(2,1)}), bf16[16,192,768]{2,1,0:T(8,128)(2,1)}) %all-gather.2.cloned.1.call-update) | async-done | bytes 4718608 | tf_op jit(solution)/shard_map/all_gather | solution.py:432
  93.4 3.5 dynamic-slice_bitcast_fusion.3
  97.1 2.7 fusion.146
  101.2 4.7 add_convert_fusion
  105.9 2.3 fusion.138
  110.9 11.5 %collective-permute-done.3 = bf16[1,2,192,768]{3,2,1,0:T(8,128)(2,1)S(1)} collective-permute-done((bf16[1,2,192,768]{3,2,1,0:T(8,128)(2,1)S(1)}, bf16[1,2,192,768]{3,2,1,0:T(8,128)(2,1)S(1)}, u32[]{:S(2)}, u32[]{:S(2)}) %collective-permute-start.3) | collective-permute-done | bytes 589856 | tf_op jit(solution)/shard_map/ppermute | solution.py:80
  122.7 33.9 %attention_forward.1 = (bf16[2560,192]{1,0:T(8,128)(2,1)}, f32[192,2560]{1,0:T(8,128)}, f32[3,2560]{1,0:T(4,128)}) custom-call(s32[4]{0:T(128)} %bitcast.160, s32[20]{0:T(128)} %fusion.109.refs_1_.origin, bf16[192,2560]{1,0:T(8,128)(2,1)} %fusion.35.refs_2_.qT, bf16[2560,384]{1,0:T(8,128)(2,1)} %get-tuple-element.175.refs_3_.kn, ...), custom_call_target="tpu_custom_call" | custom-call | flops 10066329600 | bytes 5898240 | tf_op jit(solution)/shard_map/attention_forward/pallas_call | solution.py:251
  162.3 6.2 %collective-permute-done = bf16[640,192]{1,0:T(8,128)(2,1)S(1)} collective-permute-done((bf16[640,192]{1,0:T(8,128)(2,1)S(1)}, bf16[640,192]{1,0:T(8,128)(2,1)S(1)}, u32[]{:S(2)}, u32[]{:S(2)}) %collective-permute-start) | collective-permute-done | bytes 245792 | tf_op jit(solution)/shard_map/ppermute | solution.py:500
  168.5 6.2 %collective-permute-done.2 = bf16[640,192]{1,0:T(8,128)(2,1)S(1)} collective-permute-done((bf16[640,192]{1,0:T(8,128)(2,1)S(1)}, bf16[640,192]{1,0:T(8,128)(2,1)S(1)}, u32[]{:S(2)}, u32[]{:S(2)}) %collective-permute-start.2) | collective-permute-done | bytes 245792 | tf_op jit(solution)/shard_map/ppermute | solution.py:500
  178.4 22.4 %collective-permute-done.5 = bf16[640,768]{1,0:T(8,128)(2,1)S(1)} collective-permute-done((bf16[640,768]{1,0:T(8,128)(2,1)S(1)}, bf16[640,768]{1,0:T(8,128)(2,1)S(1)}, u32[]{:S(2)}, u32[]{:S(2)}) %collective-permute-start.5) | collective-permute-done | bytes 983072 | tf_op jit(solution)/shard_map/ppermute | solution.py:80
  201.0 4.0 collective-permute-done.6
  205.0 7.8 %multiply_convert_fusion = (bf16[2560,768]{1,0:T(8,128)(2,1)S(1)}, f32[2560,768]{1,0:T(8,128)}) fusion(bf16[192,768]{1,0:T(8,128)(2,1)S(1)} %get-tuple-element.161, bf16[192,768]{1,0:T(8,128)(2,1)S(1)} %get-tuple-element.162, bf16[192,768]{1,0:T(8,128)(2,1)S(1)} %copy-done.35, bf16[192,768]{1,0:T(8,128)(2,1)S(1)} %copy-done.37, ...), kind=kOutput, calls=%fused_computation.24 | convolution fusion | flops 3054108672 | bytes 16908288 | tf_op jit(solution)/shard_map/dot_general | solution.py:39
  212.9 1.7 convolution_convert_fusion.2
  214.9 3.8 collective-permute-done.7
  222.1 22.3 %collective-permute-done.8 = bf16[640,768]{1,0:T(8,128)(2,1)S(1)} collective-permute-done((bf16[640,768]{1,0:T(8,128)(2,1)S(1)}, bf16[640,768]{1,0:T(8,128)(2,1)S(1)}, u32[]{:S(2)}, u32[]{:S(2)}) %collective-permute-start.8) | collective-permute-done | bytes 983072 | tf_op jit(solution)/shard_map/ppermute | solution.py:80
  247.2 3.3 all-to-all-start
  262.3 2.3 constant_dynamic-slice_fusion.12
  264.6 1.7 bitcast_reduce_fusion
  267.8 1.9 multiply_reduce_fusion.9
  269.7 9.1 %collective-permute-done.9 = bf16[640,768]{1,0:T(8,128)(2,1)} collective-permute-done((bf16[640,768]{1,0:T(8,128)(2,1)S(1)}, bf16[640,768]{1,0:T(8,128)(2,1)}, u32[]{:S(2)}, u32[]{:S(2)}) %collective-permute-start.9) | collective-permute-done | bytes 983072 | tf_op jit(solution)/shard_map/ppermute | solution.py:80
  278.8 2.7 pad_maximum_fusion.5
  292.4 2.3 multiply_reduce_fusion.7
  294.9 8.5 %fusion.10 = (f32[2560]{0:T(1024)S(1)}, f32[2560]{0:T(1024)S(1)}, bf16[2560,768]{1,0:T(8,128)(2,1)S(1)}) fusion(f32[768]{0:T(1024)S(1)} %get-tuple-element.133, f32[768]{0:T(1024)S(1)} %get-tuple-element.134, pred[2560]{0:T(1024)(128)(4,1)S(1)} %copy-done.65, f32[768]{0:T(1024)S(1)} %get-tuple-element.135, pred[2560]{0:T(1024)(128)(4,1)S(1)} %copy-done.66, ...), kind=kLoop, calls=%fused_computation.19 | loop fusion | flops 27520000 | bytes 7904768 | tf_op jit(solution)/shard_map/reduce_sum | solution.py:55
  303.5 4.3 fusion.13
  307.9 9.1 %fusion.9 = bf16[2560,768]{1,0:T(8,128)(2,1)S(1)} fusion(f32[2560,768]{1,0:T(8,128)S(1)} %bitcast.165, bf16[2560,768]{1,0:T(8,128)(2,1)S(1)} %fusion.13, bf16[192,768]{1,0:T(8,128)(2,1)S(1)} %copy-done.42, bf16[192,768]{1,0:T(8,128)(2,1)S(1)} %copy-done.44, bf16[192,768]{1,0:T(8,128)(2,1)S(1)} %copy-done.46, bf16[192,768]{1,0:T(8,128)(2,1)S(1)} %copy-done.40), kind=kOutput, calls=%fused_computation.18 | convolution fusion | flops 3063939072 | bytes 16908288 | tf_op jit(solution)/shard_map/dot_general | solution.py:39
  317.1 1.7 convolution_convert_fusion.1
  320.1 4.5 convolution_convert_fusion.3
  324.6 1.7 convert_add_fusion.1
  327.6 4.4 fusion.45
  332.0 18.2 %collective-permute-done.12 = bf16[640,768]{1,0:T(8,128)(2,1)S(1)} collective-permute-done((bf16[640,768]{1,0:T(8,128)(2,1)S(1)}, bf16[640,768]{1,0:T(8,128)(2,1)S(1)}, u32[]{:S(2)}, u32[]{:S(2)}) %collective-permute-start.12) | collective-permute-done | bytes 983072 | tf_op jit(solution)/shard_map/ppermute | solution.py:80
  351.1 2.9 fusion.135
  357.5 1.8 copy.162
  360.4 1.7 convolution_convert_fusion.6
  363.2 1.7 convolution_convert_fusion.5
  370.2 6.1 %collective-permute-done.15 = bf16[640,192]{1,0:T(8,128)(2,1)S(1)} collective-permute-done((bf16[640,192]{1,0:T(8,128)(2,1)}, bf16[640,192]{1,0:T(8,128)(2,1)S(1)}, u32[]{:S(2)}, u32[]{:S(2)}) %collective-permute-start.15) | collective-permute-done | bytes 245792 | tf_op jit(solution)/shard_map/ppermute | solution.py:500
  376.3 2.4 pad_maximum_fusion.11.dcn
  378.7 4.4 collective-permute-done.21
  383.3 3.0 gather_fusion.1
  386.4 4.8 broadcast_select_fusion
  391.3 48.0 %attention_backward.1 = (bf16[576,2560]{1,0:T(8,128)(2,1)}, bf16[2560,576]{1,0:T(8,128)(2,1)}, f32[3,18,128]{2,1,0:T(8,128)}) custom-call(s32[4]{0:T(128)} %bitcast.161, s32[20]{0:T(128)} %fusion.109.refs_1_.origin, bf16[192,2560]{1,0:T(8,128)(2,1)} %fusion.35.refs_2_.qT, bf16[2560,384]{1,0:T(8,128)(2,1)} %get-tuple-element.175.refs_3_.kn, ...), custom_call_target="tpu_custom_call" | custom-call | flops 25165824000 | bytes 14745600 | tf_op jit(solution)/shard_map/attention_backward/pallas_call | solution.py:374
  439.3 3.3 convolution_convert_fusion
  442.7 4.0 collective-permute-done.16
  446.7 1.7 convert_add_fusion
  450.8 3.6 convolution_convert_fusion.4
  454.4 3.6 all-to-all-start.1
  457.9 14.5 %collective-permute-done.17 = bf16[640,768]{1,0:T(8,128)(2,1)S(1)} collective-permute-done((bf16[640,768]{1,0:T(8,128)(2,1)S(1)}, bf16[640,768]{1,0:T(8,128)(2,1)S(1)}, u32[]{:S(2)}, u32[]{:S(2)}) %collective-permute-start.17) | collective-permute-done | bytes 983072 | tf_op jit(solution)/shard_map/ppermute | solution.py:80
  472.4 3.3 fusion.23
  475.7 2.6 fusion.20
  485.7 1.8 fusion.115
  490.5 11.0 %collective-permute-done.18 = bf16[640,768]{1,0:T(8,128)(2,1)S(1)} collective-permute-done((bf16[640,768]{1,0:T(8,128)(2,1)S(1)}, bf16[640,768]{1,0:T(8,128)(2,1)S(1)}, u32[]{:S(2)}, u32[]{:S(2)}) %collective-permute-start.18) | collective-permute-done | bytes 983072 | tf_op jit(solution)/shard_map/ppermute | solution.py:80
  502.9 1.9 fusion.53
  506.5 2.6 all-to-all-start.3
  509.1 38.1 %all_gather.7 = bf16[576,768]{1,0:T(8,128)(2,1)S(1)} all-gather(bf16[72,768]{1,0:T(8,128)(2,1)S(1)} %get-tuple-element.195), channel_id=1, replica_groups=mesh['wide'=8,'narrow'=4] {'wide'}, dimensions={0}, use_global_device_ids=true | all-gather | bytes 995328 | tf_op jit(solution)/shard_map/all_gather | solution.py:662
  550.0 2.1 pad_maximum_fusion.2
  552.7 1.8 constant_dynamic-slice_fusion.3
  554.5 3.5 maximum_convert_fusion.1
  557.9 2.0 multiply_reduce_fusion.5
  561.9 2.6 all-to-all-start.2
  564.6 4.9 maximum_convert_fusion
  569.5 3.2 all-to-all-done.2
  577.7 4.9 multiply_subtract_fusion
  (361 shorter events, 79.4 us)
Async XLA Ops:
  7.2 19.5 %copy-start.93 = (s32[1,4]{1,0:T(1,128)S(1)}, s32[1,4]{1,0:T(1,128)}, u32[]{:S(2)}) copy-start(s32[1,4]{1,0:T(1,128)} %param.23) | copy-start | bytes 52
  7.2 19.7 %copy-start.73 = (s32[2047]{0:T(1024)S(1)}, s32[2047]{0:T(1024)}, u32[]{:S(2)}) copy-start(s32[2047]{0:T(1024)} %param.24) | copy-start | bytes 24568
  7.2 20.5 %copy-start.80 = (f32[32,3]{0,1:T(4,128)S(1)}, f32[32,3]{0,1:T(4,128)}, u32[]{:S(2)}) copy-start(f32[32,3]{0,1:T(4,128)} %param.32) | copy-start | bytes 1156
  7.2 86.2 %all-gather.2.cloned.1.call-start = ((), (), s32[]{:S(2)}) async-start(), calls=%async_computation.5 | async-start | bytes 5308416 | tf_op jit(solution)/shard_map/all_gather | solution.py:432
  30.0 14.4 %copy-start.54 = (f32[3,768]{1,0:T(4,128)S(1)}, f32[3,768]{1,0:T(4,128)}, u32[]{:S(2)}) copy-start(f32[3,768]{1,0:T(4,128)} %param.29) | copy-start | bytes 27652
  45.0 56.2 %copy-start.62 = (f32[768]{0:T(1024)}, f32[768]{0:T(1024)S(1)}, u32[]{:S(2)}) copy-start(f32[768]{0:T(1024)S(1)} %get-tuple-element.138) | copy-start | bytes 9220
  48.2 53.1 %copy-start.68 = (f32[2560]{0:T(1024)}, f32[2560]{0:T(1024)S(1)}, u32[]{:S(2)}) copy-start(f32[2560]{0:T(1024)S(1)} %add_rsqrt_fusion.1) | copy-start | bytes 30724
  97.0 108.0 %copy-start.31 = (bf16[192,768]{1,0:T(8,128)(2,1)}, bf16[192,768]{1,0:T(8,128)(2,1)S(1)}, u32[]{:S(2)}) copy-start(bf16[192,768]{1,0:T(8,128)(2,1)S(1)} %get-tuple-element.161) | copy-start | bytes 884740
  97.0 108.0 %copy-start.33 = (bf16[192,768]{1,0:T(8,128)(2,1)}, bf16[192,768]{1,0:T(8,128)(2,1)S(1)}, u32[]{:S(2)}) copy-start(bf16[192,768]{1,0:T(8,128)(2,1)S(1)} %get-tuple-element.162) | copy-start | bytes 884740
  108.3 14.1 %collective-permute-start.3 = (bf16[1,2,192,768]{3,2,1,0:T(8,128)(2,1)S(1)}, bf16[1,2,192,768]{3,2,1,0:T(8,128)(2,1)S(1)}, u32[]{:S(2)}, u32[]{:S(2)}) collective-permute-start(bf16[1,2,192,768]{3,2,1,0:T(8,128)(2,1)S(1)} %maximum_bitcast_fusion), channel_id=1, source_target_pairs={{0,2},{1,3},{2,0},{3,1},{4,6},{5,7},{6,4},{7,5},{8,10},{9,11},{10,... | collective-permute-start | bytes 1769480 | tf_op jit(solution)/shard_map/ppermute | solution.py:80
  122.5 37.7 %copy-start.13 = (bf16[1,2,192,768]{3,2,1,0:T(8,128)(2,1)}, bf16[1,2,192,768]{3,2,1,0:T(8,128)(2,1)S(1)}, u32[]{:S(2)}) copy-start(bf16[1,2,192,768]{3,2,1,0:T(8,128)(2,1)S(1)} %collective-permute-done.3) | copy-start | bytes 1769476
  122.6 37.6 %collective-permute-start.4 = (bf16[2,2,192,768]{3,2,1,0:T(8,128)(2,1)S(1)}, bf16[2,2,192,768]{3,2,1,0:T(8,128)(2,1)S(1)}, u32[]{:S(2)}, u32[]{:S(2)}) collective-permute-start(bf16[2,2,192,768]{3,2,1,0:T(8,128)(2,1)S(1)} %pad_maximum_fusion.12), channel_id=1, source_target_pairs={{0,1},{1,0},{2,3},{3,2},{4,5},{5,4},{6,7},{7,6},{8,9},{9,8},{10,11... | collective-permute-start | bytes 3538952 | tf_op jit(solution)/shard_map/ppermute | solution.py:80
  157.9 16.8 %copy-start.27 = (bf16[640,192]{1,0:T(8,128)(2,1)}, bf16[640,192]{1,0:T(8,128)(2,1)S(1)}, u32[]{:S(2)}) copy-start(bf16[640,192]{1,0:T(8,128)(2,1)S(1)} %get-tuple-element.184) | copy-start | bytes 737284
  157.9 10.6 %collective-permute-start = (bf16[640,192]{1,0:T(8,128)(2,1)S(1)}, bf16[640,192]{1,0:T(8,128)(2,1)S(1)}, u32[]{:S(2)}, u32[]{:S(2)}) collective-permute-start(bf16[640,192]{1,0:T(8,128)(2,1)S(1)} %get-tuple-element.187), channel_id=1, source_target_pairs={{0,2},{1,3},{2,0},{3,1},{4,6},{5,7},{6,4},{7,5},{8,10},{9,11},{10,... | collective-permute-start | bytes 737288 | tf_op jit(solution)/shard_map/ppermute | solution.py:500
  159.5 9.0 %collective-permute-start.1 = (bf16[640,192]{1,0:T(8,128)(2,1)S(1)}, bf16[640,192]{1,0:T(8,128)(2,1)S(1)}, u32[]{:S(2)}, u32[]{:S(2)}) collective-permute-start(bf16[640,192]{1,0:T(8,128)(2,1)S(1)} %get-tuple-element.186), channel_id=1, source_target_pairs={{0,1},{1,0},{2,3},{3,2},{4,5},{5,4},{6,7},{7,6},{8,9},{9,8},{10,11... | collective-permute-start | bytes 737288 | tf_op jit(solution)/shard_map/ppermute | solution.py:500
  159.7 15.0 %collective-permute-start.2 = (bf16[640,192]{1,0:T(8,128)(2,1)S(1)}, bf16[640,192]{1,0:T(8,128)(2,1)S(1)}, u32[]{:S(2)}, u32[]{:S(2)}) collective-permute-start(bf16[640,192]{1,0:T(8,128)(2,1)S(1)} %get-tuple-element.185), channel_id=1, source_target_pairs={{0,3},{1,2},{2,1},{3,0},{4,7},{5,6},{6,5},{7,4},{8,11},{9,10},{10,... | collective-permute-start | bytes 737288 | tf_op jit(solution)/shard_map/ppermute | solution.py:500
  175.8 68.5 %copy-start.3 = (f32[640,768]{1,0:T(8,128)}, f32[640,768]{1,0:T(8,128)S(1)}, u32[]{:S(2)}) copy-start(f32[640,768]{1,0:T(8,128)S(1)} %get-tuple-element.227) | copy-start | bytes 5898244
  176.8 36.1 %copy-start.10 = (bf16[640,768]{1,0:T(8,128)(2,1)}, bf16[640,768]{1,0:T(8,128)(2,1)S(1)}, u32[]{:S(2)}) copy-start(bf16[640,768]{1,0:T(8,128)(2,1)S(1)} %multiply_convert_fusion.1) | copy-start | bytes 2949124
  176.8 28.2 %copy-start.35 = (bf16[192,768]{1,0:T(8,128)(2,1)S(1)}, bf16[192,768]{1,0:T(8,128)(2,1)}, u32[]{:S(2)}) copy-start(bf16[192,768]{1,0:T(8,128)(2,1)} %get-tuple-element.163) | copy-start | bytes 884740
  176.8 28.2 %copy-start.37 = (bf16[192,768]{1,0:T(8,128)(2,1)S(1)}, bf16[192,768]{1,0:T(8,128)(2,1)}, u32[]{:S(2)}) copy-start(bf16[192,768]{1,0:T(8,128)(2,1)} %get-tuple-element.164) | copy-start | bytes 884740
  176.8 24.0 %collective-permute-start.5 = (bf16[640,768]{1,0:T(8,128)(2,1)S(1)}, bf16[640,768]{1,0:T(8,128)(2,1)S(1)}, u32[]{:S(2)}, u32[]{:S(2)}) collective-permute-start(bf16[640,768]{1,0:T(8,128)(2,1)S(1)} %multiply_convert_fusion.1), channel_id=1, source_target_pairs={{0,2},{1,3},{2,0},{3,1},{4,6},{5,7},{6,4},{7,5},{8,10},{9,11},{10,... | collective-permute-start | bytes 2949128 | tf_op jit(solution)/shard_map/ppermute | solution.py:80
  200.8 12.1 %copy-start.22 = (bf16[640,768]{1,0:T(8,128)(2,1)}, bf16[640,768]{1,0:T(8,128)(2,1)S(1)}, u32[]{:S(2)}) copy-start(bf16[640,768]{1,0:T(8,128)(2,1)S(1)} %collective-permute-done.5) | copy-start | bytes 2949124
  200.9 4.0 collective-permute-start.6
  214.7 4.0 collective-permute-start.7
  220.5 23.9 %collective-permute-start.8 = (bf16[640,768]{1,0:T(8,128)(2,1)S(1)}, bf16[640,768]{1,0:T(8,128)(2,1)S(1)}, u32[]{:S(2)}, u32[]{:S(2)}) collective-permute-start(bf16[640,768]{1,0:T(8,128)(2,1)S(1)} %slice.494), channel_id=1, source_target_pairs={{0,2},{1,3},{2,0},{3,1},{4,6},{5,7},{6,4},{7,5},{8,10},{9,11},{10,... | collective-permute-start | bytes 2949128 | tf_op jit(solution)/shard_map/ppermute | solution.py:80
  222.1 22.9 %copy-start.82 = (f32[4]{0:T(128)}, f32[4]{0:T(128)S(1)}, u32[]{:S(2)}) copy-start(f32[4]{0:T(128)S(1)} %bitcast_convert_fusion) | copy-start | bytes 52
  247.2 17.3 %all-to-all-start = ((f32[32,4,768]{2,1,0:T(4,128)}), f32[32,4,768]{2,1,0:T(4,128)}, u32[]{:S(2)}, u32[]{:S(2)}) async-start(f32[32,4,768]{2,1,0:T(4,128)} %broadcast_in_dim.211), calls=%async_computation | async-start | bytes 786432 | tf_op jit(solution)/shard_map/all_to_all | solution.py:138
  250.5 307.4 %reduce-scatter.2.cloned.1.call-start = ((), (), s32[]{:S(2)}) async-start(), calls=%async_computation.6 | async-start | bytes 5308416 | tf_op jit(solution)/shard_map/reduce_scatter | solution.py:647
  251.0 27.8 %collective-permute-start.9 = (bf16[640,768]{1,0:T(8,128)(2,1)S(1)}, bf16[640,768]{1,0:T(8,128)(2,1)}, u32[]{:S(2)}, u32[]{:S(2)}) collective-permute-start(bf16[640,768]{1,0:T(8,128)(2,1)S(1)} %get-tuple-element.153), channel_id=1, source_target_pairs={{0,2},{1,3},{2,0},{3,1},{4,6},{5,7},{6,4},{7,5},{8,10},{9,11},{10,... | collective-permute-start | bytes 2949128 | tf_op jit(solution)/shard_map/ppermute | solution.py:80
  269.7 11.8 %copy-start.25 = (f32[32,768]{1,0:T(8,128)}, f32[32,768]{1,0:T(8,128)S(1)}, u32[]{:S(2)}) copy-start(f32[32,768]{1,0:T(8,128)S(1)} %get-tuple-element.231) | copy-start | bytes 294916
  281.5 13.3 %collective-permute-start.10 = (bf16[1280,768]{1,0:T(8,128)(2,1)}, bf16[1280,768]{1,0:T(8,128)(2,1)}, u32[]{:S(2)}, u32[]{:S(2)}) collective-permute-start(bf16[1280,768]{1,0:T(8,128)(2,1)} %pad_maximum_fusion.5), channel_id=1, source_target_pairs={{0,1},{1,0},{2,3},{3,2},{4,5},{5,4},{6,7},{7,6},{8,9},{9,8},{10,11... | collective-permute-start | bytes 5898248 | tf_op jit(solution)/shard_map/ppermute | solution.py:80
  292.4 15.4 %slice-start = ((s8[7864320]{0:T(1024)(128)(4,1)}), s8[4194304]{0:T(1024)(128)(4,1)S(1)}, s32[]{:S(2)}) async-start(s8[7864320]{0:T(1024)(128)(4,1)} %bitcast.164), calls=%async_computation.7 | async-start | bytes 8388608
  294.9 12.8 %slice-start.1 = ((s8[7864320]{0:T(1024)(128)(4,1)}), s8[3670016]{0:T(1024)(128)(4,1)S(1)}, s32[]{:S(2)}) async-start(s8[7864320]{0:T(1024)(128)(4,1)} %bitcast.164), calls=%async_computation.8 | async-start | bytes 7340032
  318.8 5.8 collective-permute-start.11
  326.5 23.8 %copy-start.4 = (f32[640,768]{1,0:T(8,128)S(1)}, f32[640,768]{1,0:T(8,128)}, u32[]{:S(2)}) copy-start(f32[640,768]{1,0:T(8,128)} %copy-done.3) | copy-start | bytes 5898244
  326.5 23.8 %copy-start.51 = (f32[640]{0:T(1024)S(1)}, f32[640]{0:T(1024)}, u32[]{:S(2)}) copy-start(f32[640]{0:T(1024)} %copy-done.50) | copy-start | bytes 7684
  326.5 23.8 %copy-start.53 = (f32[768]{0:T(1024)S(1)}, f32[768]{0:T(1024)}, u32[]{:S(2)}) copy-start(f32[768]{0:T(1024)} %get-tuple-element.137) | copy-start | bytes 9220
  326.5 23.8 %collective-permute-start.12 = (bf16[640,768]{1,0:T(8,128)(2,1)S(1)}, bf16[640,768]{1,0:T(8,128)(2,1)S(1)}, u32[]{:S(2)}, u32[]{:S(2)}) collective-permute-start(bf16[640,768]{1,0:T(8,128)(2,1)S(1)} %slice.493), channel_id=1, source_target_pairs={{0,2},{1,3},{2,0},{3,1},{4,6},{5,7},{6,4},{7,5},{8,10},{9,11},{10,... | collective-permute-start | bytes 2949128 | tf_op jit(solution)/shard_map/ppermute | solution.py:80
  332.0 19.0 %copy-start.57 = (f32[640]{0:T(1024)S(1)}, f32[640]{0:T(1024)}, u32[]{:S(2)}) copy-start(f32[640]{0:T(1024)} %copy-done.56) | copy-start | bytes 7684
  356.1 10.7 %collective-permute-start.20 = (bf16[384,768]{1,0:T(8,128)(2,1)S(1)}, bf16[384,768]{1,0:T(8,128)(2,1)}, u32[]{:S(2)}, u32[]{:S(2)}) collective-permute-start(bf16[384,768]{1,0:T(8,128)(2,1)S(1)} %slice.495), channel_id=1, source_target_pairs={{0,1},{1,0},{2,3},{3,2},{4,5},{5,4},{6,7},{7,6},{8,9},{9,8},{10,11... | collective-permute-start | bytes 1769480 | tf_op jit(solution)/shard_map/ppermute | solution.py:80
  359.4 10.8 %collective-permute-start.13 = (bf16[640,192]{1,0:T(8,128)(2,1)}, bf16[640,192]{1,0:T(8,128)(2,1)}, u32[]{:S(2)}, u32[]{:S(2)}) collective-permute-start(bf16[640,192]{1,0:T(8,128)(2,1)} %copy.162), channel_id=1, source_target_pairs={{0,2},{1,3},{2,0},{3,1},{4,6},{5,7},{6,4},{7,5},{8,10},{9,11},{10,... | collective-permute-start | bytes 737288 | tf_op jit(solution)/shard_map/ppermute | solution.py:500
  363.1 7.1 %collective-permute-start.14 = (bf16[640,192]{1,0:T(8,128)(2,1)}, bf16[640,192]{1,0:T(8,128)(2,1)}, u32[]{:S(2)}, u32[]{:S(2)}) collective-permute-start(bf16[640,192]{1,0:T(8,128)(2,1)} %copy.163), channel_id=1, source_target_pairs={{0,1},{1,0},{2,3},{3,2},{4,5},{5,4},{6,7},{7,6},{8,9},{9,8},{10,11... | collective-permute-start | bytes 737288 | tf_op jit(solution)/shard_map/ppermute | solution.py:500
  365.9 10.4 %collective-permute-start.15 = (bf16[640,192]{1,0:T(8,128)(2,1)}, bf16[640,192]{1,0:T(8,128)(2,1)S(1)}, u32[]{:S(2)}, u32[]{:S(2)}) collective-permute-start(bf16[640,192]{1,0:T(8,128)(2,1)} %copy.164), channel_id=1, source_target_pairs={{0,3},{1,2},{2,1},{3,0},{4,7},{5,6},{6,5},{7,4},{8,11},{9,10},{10,... | collective-permute-start | bytes 737288 | tf_op jit(solution)/shard_map/ppermute | solution.py:500
  368.0 15.1 %copy-start.20 = (bf16[768,768]{1,0:T(8,128)(2,1)S(1)}, bf16[768,768]{1,0:T(8,128)(2,1)}, u32[]{:S(2)}) copy-start(bf16[768,768]{1,0:T(8,128)(2,1)} %fusion.45) | copy-start | bytes 3538948
  368.0 15.0 %collective-permute-start.21 = (bf16[192,768]{1,0:T(8,128)(2,1)S(1)}, bf16[192,768]{1,0:T(8,128)(2,1)S(1)}, u32[]{:S(2)}, u32[]{:S(2)}) collective-permute-start(bf16[192,768]{1,0:T(8,128)(2,1)S(1)} %slice.496), channel_id=1, source_target_pairs={{0,2},{1,3},{2,0},{3,1},{4,6},{5,7},{6,4},{7,5},{8,10},{9,11},{10,... | collective-permute-start | bytes 884744 | tf_op jit(solution)/shard_map/ppermute | solution.py:80
  391.2 48.0 %copy-start.16 = (bf16[192,768]{1,0:T(8,128)(2,1)S(1)}, bf16[192,768]{1,0:T(8,128)(2,1)}, u32[]{:S(2)}) copy-start(bf16[192,768]{1,0:T(8,128)(2,1)} %copy-done.15) | copy-start | bytes 884740
  391.2 48.0 %copy-start.18 = (bf16[192,768]{1,0:T(8,128)(2,1)S(1)}, bf16[192,768]{1,0:T(8,128)(2,1)}, u32[]{:S(2)}) copy-start(bf16[192,768]{1,0:T(8,128)(2,1)} %copy-done.17) | copy-start | bytes 884740
  391.2 48.0 %copy-start.30 = (bf16[192,768]{1,0:T(8,128)(2,1)S(1)}, bf16[192,768]{1,0:T(8,128)(2,1)}, u32[]{:S(2)}) copy-start(bf16[192,768]{1,0:T(8,128)(2,1)} %copy-done.29) | copy-start | bytes 884740
  442.6 4.0 collective-permute-start.16
  448.5 23.9 %collective-permute-start.17 = (bf16[640,768]{1,0:T(8,128)(2,1)S(1)}, bf16[640,768]{1,0:T(8,128)(2,1)S(1)}, u32[]{:S(2)}, u32[]{:S(2)}) collective-permute-start(bf16[640,768]{1,0:T(8,128)(2,1)S(1)} %slice.492), channel_id=1, source_target_pairs={{0,2},{1,3},{2,0},{3,1},{4,6},{5,7},{6,4},{7,5},{8,10},{9,11},{10,... | collective-permute-start | bytes 2949128 | tf_op jit(solution)/shard_map/ppermute | solution.py:80
  454.4 50.5 %all-to-all-start.1 = ((bf16[8,72,768]{2,1,0:T(8,128)(2,1)}), bf16[8,72,768]{2,1,0:T(8,128)(2,1)S(1)}, u32[]{:S(2)}, u32[]{:S(2)}) async-start(bf16[8,72,768]{2,1,0:T(8,128)(2,1)} %bitcast.157), calls=%async_computation.2 | async-start | bytes 1769472 | tf_op jit(solution)/shard_map/all_to_all | solution.py:654
  457.9 17.7 %copy-start.7 = (f32[640,768]{1,0:T(8,128)S(1)}, f32[640,768]{1,0:T(8,128)}, u32[]{:S(2)}) copy-start(f32[640,768]{1,0:T(8,128)} %get-tuple-element.151) | copy-start | bytes 5898244
  475.7 13.7 %copy-start.26 = (f32[32,768]{1,0:T(8,128)S(1)}, f32[32,768]{1,0:T(8,128)}, u32[]{:S(2)}) copy-start(f32[32,768]{1,0:T(8,128)} %reshape.404) | copy-start | bytes 294916
  475.7 13.7 %copy-start.61 = (f32[768]{0:T(1024)S(1)}, f32[768]{0:T(1024)}, u32[]{:S(2)}) copy-start(f32[768]{0:T(1024)} %get-tuple-element.136) | copy-start | bytes 9220
  478.3 23.1 %collective-permute-start.18 = (bf16[640,768]{1,0:T(8,128)(2,1)S(1)}, bf16[640,768]{1,0:T(8,128)(2,1)S(1)}, u32[]{:S(2)}, u32[]{:S(2)}) collective-permute-start(bf16[640,768]{1,0:T(8,128)(2,1)S(1)} %fusion.20), channel_id=1, source_target_pairs={{0,2},{1,3},{2,0},{3,1},{4,6},{5,7},{6,4},{7,5},{8,10},{9,11},{10,... | collective-permute-start | bytes 2949128 | tf_op jit(solution)/shard_map/ppermute | solution.py:80
  490.5 15.2 %copy-start.67 = (f32[768]{0:T(1024)S(1)}, f32[768]{0:T(1024)}, u32[]{:S(2)}) copy-start(f32[768]{0:T(1024)} %get-tuple-element.124) | copy-start | bytes 9220
  502.9 47.1 %collective-permute-start.19 = (bf16[1280,768]{1,0:T(8,128)(2,1)}, bf16[1280,768]{1,0:T(8,128)(2,1)}, u32[]{:S(2)}, u32[]{:S(2)}) collective-permute-start(bf16[1280,768]{1,0:T(8,128)(2,1)} %pad_maximum_fusion.6), channel_id=1, source_target_pairs={{0,1},{1,0},{2,3},{3,2},{4,5},{5,4},{6,7},{7,6},{8,9},{9,8},{10,11... | collective-permute-start | bytes 5898248 | tf_op jit(solution)/shard_map/ppermute | solution.py:80
  506.5 42.0 %all-to-all-start.3 = ((f32[32,3,768]{2,1,0:T(4,128)}), f32[32,3,768]{2,1,0:T(4,128)S(1)}, u32[]{:S(2)}, u32[]{:S(2)}) async-start(f32[32,3,768]{2,1,0:T(4,128)} %broadcast_in_dim.230), calls=%async_computation.4 | async-start | bytes 786432 | tf_op jit(solution)/shard_map/all_to_all | solution.py:138
  561.9 10.8 %all-to-all-start.2 = ((f32[32,8,128]{2,1,0:T(8,128)}), f32[32,8,128]{2,1,0:T(8,128)S(1)}, u32[]{:S(2)}, u32[]{:S(2)}) async-start(f32[32,8,128]{2,1,0:T(8,128)} %broadcast_in_dim_broadcast_in_dim_broadcast_in_dim.3), calls=%async_computation.3 | async-start | bytes 262144 | tf_op jit(solution)/shard_map/all_to_all | solution.py:138
  564.6 11.8 %copy-start.81 = (f32[32,3]{0,1:T(4,128)S(1)}, f32[32,3]{0,1:T(4,128)}, u32[]{:S(2)}) copy-start(f32[32,3]{0,1:T(4,128)} %param.32) | copy-start | bytes 1156
  564.6 13.1 %copy-start.9 = (f32[2,192,768]{2,1,0:T(8,128)S(1)}, f32[2,192,768]{2,1,0:T(8,128)}, u32[]{:S(2)}) copy-start(f32[2,192,768]{2,1,0:T(8,128)} %param.26) | copy-start | bytes 3538948
  564.6 13.1 %copy-start.12 = (bf16[2,192,768]{2,1,0:T(8,128)(2,1)S(1)}, bf16[2,192,768]{2,1,0:T(8,128)(2,1)}, u32[]{:S(2)}) copy-start(bf16[2,192,768]{2,1,0:T(8,128)(2,1)} %reduce-scatter.2.cloned.1.call-done) | copy-start | bytes 1769476
  564.6 13.1 %copy-start.78 = (pred[2]{0:T(512)(128)(4,1)S(1)}, pred[2]{0:T(512)(128)(4,1)}, u32[]{:S(2)}) copy-start(pred[2]{0:T(512)(128)(4,1)} %get-tuple-element.240) | copy-start | bytes 10
  564.6 13.1 %copy-start.79 = (pred[2]{0:T(512)(128)(4,1)S(1)}, pred[2]{0:T(512)(128)(4,1)}, u32[]{:S(2)}) copy-start(pred[2]{0:T(512)(128)(4,1)} %get-tuple-element.241) | copy-start | bytes 10
  (66 other events, 320.8 us)
Sparse Core Ops, SparseCore 0:
  10.8 82.5 all-gather.1
  391.3 109.3 reduce-scatter.1
